TPU v7x, 32 devices: a whole 2x2x4 slice. The times are simulated.
32 devices in a mesh: dp: 16 (over z, y, x), mp: 2 (over core).
Axes of the slice: x: 2, y: 2, z: 4, core: 2. Of those that a mesh axis runs over, the one named last changes fastest.
Arguments:
- pool_images: bfloat16 [128, 196, 768], P('dp'), may hold values from -6 to 6
- pick_rows: int32 [128], P('dp'), may hold values from 0 to 7
- pick_weight: int32 [128], P('dp'), may hold values from 1 to 8
- pick_label: int32 [128], P('dp'), may hold values from 0 to 999
- in_proj: float32 [2, 384, 1152], P('mp', None, 'dp'), may hold values from -0.3125 to 0.3125
- out_proj: float32 [2, 384, 384], P('mp', None, 'dp'), may hold values from -2 to 2
- up_proj: float32 [2, 384, 1536], P('mp', None, 'dp'), may hold values from -0.3125 to 0.3125
- down_proj: float32 [2, 384, 1536], P('mp', None, 'dp'), may hold values from -0.15625 to 0.15625
- in_moment: float32 [2, 384, 1152], P('mp', None, 'dp'), may hold values from -3.0517578e-05 to 3.0517578e-05
- out_moment: float32 [2, 384, 384], P('mp', None, 'dp'), may hold values from -3.0517578e-05 to 3.0517578e-05
- up_moment: float32 [2, 384, 1536], P('mp', None, 'dp'), may hold values from -3.0517578e-05 to 3.0517578e-05
- down_moment: float32 [2, 384, 1536], P('mp', None, 'dp'), may hold values from -3.0517578e-05 to 3.0517578e-05
- patch_embed: float32 [768, 384], P('dp'), may hold values from -0.21875 to 0.21875
- class_head: float32 [384, 1000], P('dp'), may hold values from -0.625 to 0.625
- pos_table: float32 [384, 197], P('dp'), may hold values from -3 to 3
- norm_params: float32 [384, 10], P('dp'), may hold values from -1 to 4, as said below
- patch_first: float32 [768, 384], P('dp'), may hold values from -3.33786e-06 to 3.33786e-06
- head_first: float32 [384, 1000], P('dp'), may hold values from -3.33786e-06 to 3.33786e-06
- pos_first: float32 [384, 197], P('dp'), may hold values from -3.33786e-06 to 3.33786e-06
- norm_first: float32 [384, 10], P('dp'), may hold values from -1.335144e-05 to 1.335144e-05
- patch_second: float32 [768, 384], P('dp'), may hold values from 1.23332e-12 to 4.93328e-12
- head_second: float32 [384, 1000], P('dp'), may hold values from 1.23332e-12 to 4.93328e-12
- pos_second: float32 [384, 197], P('dp'), may hold values from 1.23332e-12 to 4.93328e-12
- norm_second: float32 [384, 10], P('dp'), may hold values from 1.9779659e-11 to 7.9118635e-11
Outputs:
- loss_total: float32 [], replicated
- weight_total: float32 [], replicated
- grad_norm: float32 [], replicated
- pool_score: float32 [128], P(('dp', 'mp'))
- new_in_proj: float32 [2, 384, 1152], P('mp', None, 'dp')
- new_out_proj: float32 [2, 384, 384], P('mp', None, 'dp')
- new_up_proj: float32 [2, 384, 1536], P('mp', None, 'dp')
- new_down_proj: float32 [2, 384, 1536], P('mp', None, 'dp')
- new_in_moment: float32 [2, 384, 1152], P('mp', None, 'dp')
- new_out_moment: float32 [2, 384, 384], P('mp', None, 'dp')
- new_up_moment: float32 [2, 384, 1536], P('mp', None, 'dp')
- new_down_moment: float32 [2, 384, 1536], P('mp', None, 'dp')
- new_patch_embed: float32 [768, 384], P('dp')
- new_class_head: float32 [384, 1000], P('dp')
- new_pos_table: float32 [384, 197], P('dp')
- new_norm_params: float32 [384, 10], P('dp')
- new_patch_first: float32 [768, 384], P('dp')
- new_head_first: float32 [384, 1000], P('dp')
- new_pos_first: float32 [384, 197], P('dp')
- new_norm_first: float32 [384, 10], P('dp')
- new_patch_second: float32 [768, 384], P('dp')
- new_head_second: float32 [384, 1000], P('dp')
- new_pos_second: float32 [384, 197], P('dp')
- new_norm_second: float32 [384, 10], P('dp')
Inputs may be any that keep to these rules, and one draw needn't show every extreme that they name: `pick_rows`: an index into the 8 pool images of the same block of dp. `norm_params`: even columns are gains, positive; odd columns are biases.
All inputs are finite; a program needn't handle non-finite values.
Results may differ from a plain program's by a relative error of at most 0.0095.
The roundings to bfloat16 on the way count: a program that leaves them out, or rounds other values in their place, can miss the bound.
Values may be sent and summed in bfloat16 or wider, within the bound.
A program may use at most 256 MiB of HBM per device.

v0:
```python
import math

import jax
import jax.numpy as jnp
from jax import lax
from jax.experimental import pallas as pl
from jax.experimental.pallas import tpu as pltpu
from jax.sharding import PartitionSpec as P

HEAD_DIM = 64
STEP = 5
EPSILON = 1e-06
NS_A = 3.4445
NS_B = -4.775
NS_C = 2.0315
MOMENTUM = 0.95
MUON_RATES = (0.1, 0.4, 0.1, 0.1)
DECAY = 0.01
BETA_ONE = 0.9
BETA_TWO = 0.95
ADAM_EPS = 1e-08
ADAM_RATES = (0.01, 0.02, 0.1, 0.2)
THRESHOLD = 0.01
PRECISE = lax.Precision.HIGHEST
BF = jnp.bfloat16
FL = jnp.float32


def layer_norm(values, gain, bias):
    centered = values - jnp.mean(values, -1, keepdims=True)
    inverse = lax.rsqrt(jnp.mean(centered * centered, -1, keepdims=True) + EPSILON)
    unit = centered * inverse
    return (unit * gain + bias, unit, inverse)


def layer_norm_grad(upstream, unit, inverse, gain):
    axes = tuple(range(upstream.ndim - 1))
    d_gain = jnp.sum(upstream * unit, axes)
    d_bias = jnp.sum(upstream, axes)
    scaled = upstream * gain
    d_values = inverse * (
        scaled
        - jnp.mean(scaled, -1, keepdims=True)
        - unit * jnp.mean(scaled * unit, -1, keepdims=True)
    )
    return (d_values, d_gain, d_bias)


def gelu(values):
    return 0.5 * values * (1.0 + lax.erf(values * math.sqrt(0.5)))


def gelu_slope(values):
    bell = math.sqrt(0.5 / math.pi) * jnp.exp(-0.5 * values * values)
    return 0.5 * (1.0 + lax.erf(values * math.sqrt(0.5))) + values * bell


def dot(formula, left, right):
    return jnp.einsum(formula, left, right, preferred_element_type=FL)


MESH = pl.DeviceIdType.MESH
LINE = 4
GRID_DP = 16
SHARE = 96
FETCH_SLOTS = (0, 8, 16, 24)
JOB_SLOTS = (0, 10, 18)


def place():
    k = lax.axis_index("dp")
    c = lax.axis_index("mp")
    z = k // 4
    y = (k // 2) % 2
    x = k % 2
    return (k, c, z, y, x, k + 2 - 4 * y, k + 1 - 2 * x)


def greet(k, c, z, y_peer, x_peer):
    barrier = pltpu.get_barrier_semaphore()

    def signal(dp, mp):
        pl.semaphore_signal(barrier, inc=1, device_id=(dp, mp), device_id_type=MESH)

    signal(k, 1 - c)
    signal(y_peer, c)
    signal(x_peer, c)

    @pl.when(z > 0)
    def _():
        signal(k - 4, c)

    @pl.when(z < LINE - 1)
    def _():
        signal(k + 4, c)

    peers = 3 + jnp.minimum(z, 1) + jnp.minimum(LINE - 1 - z, 1)
    pl.semaphore_wait(barrier, peers)


def gather_weights(mats, patch_embed, class_head, pos_table, norm_params):
    dp_size = lax.axis_size("dp")
    mp_size = lax.axis_size("mp")
    mp_index = lax.axis_index("mp")
    counts = [mat.shape[2] for mat in mats]
    width = mats[0].shape[1]
    classes = class_head.shape[1]
    tokens = pos_table.shape[1]
    head_rows, head_parts = class_head.shape[0], -(-classes // width)
    head = jnp.pad(class_head, ((0, 0), (0, head_parts * width - classes)))
    head = [head[:, part * width : (part + 1) * width] for part in range(head_parts)]
    matrix_rows = sum(counts)
    patch_rows = patch_embed.shape[0]
    total = matrix_rows + max(patch_rows + head_rows, head_rows * head_parts) + 8
    lead = [mat[0].T for mat in mats]

    def filled(parts):
        rows = sum([part.shape[0] for part in parts])
        return jnp.concatenate(parts + [jnp.zeros((total - rows, width), FL)], 0).astype(BF)

    packed = jnp.where(mp_index == 0, filled(lead + [patch_embed]), filled(lead + head))
    both = jnp.concatenate([pos_table, norm_params], 1)
    both = jnp.pad(both, ((0, 0), (0, 128 * mp_size - both.shape[1])))
    both = lax.dynamic_slice_in_dim(both, mp_index * 128, 128, 1)
    whole = lax.all_gather(packed, ("dp", "mp"))
    whole = jnp.swapaxes(whole.reshape((dp_size, mp_size) + packed.shape), 0, 1)
    table = lax.all_gather(both, ("dp", "mp"))
    table = jnp.swapaxes(table.reshape((dp_size, mp_size) + both.shape), 0, 1)
    return (whole, table)


def unpack_weights(whole, table, mats, patch_embed, class_head, pos_table, norm_params):
    mp_size, dp_size = whole.shape[:2]
    counts = [mat.shape[2] for mat in mats]
    width = whole.shape[3]
    classes = class_head.shape[1]
    tokens = pos_table.shape[1]
    head_rows, head_parts = class_head.shape[0], -(-classes // width)
    patch_rows = patch_embed.shape[0]
    parts = []
    at = 0
    for count in counts:
        parts.append(whole[:, :, at : at + count].reshape(mp_size, dp_size * count, width))
        at += count
    patch_w = whole[0, :, at : at + patch_rows].reshape(dp_size * patch_rows, width)
    head_w = [
        whole[1, :, at + part * head_rows : at + (part + 1) * head_rows].reshape(width, width)
        for part in range(head_parts)
    ]
    head_w = jnp.concatenate(head_w, 1)[:, :classes]
    table = jnp.concatenate([table[0], table[1]], -1).reshape(width, 128 * mp_size).T
    return (parts, patch_w, head_w, table[:tokens], table[tokens : tokens + norm_params.shape[1]])


def local_step(images, counts, target_weight, fetched):
    (in_t, out_t, up_t, down_t), patch_w, head_w, pos_t, norm_t = fetched
    image_count = images.shape[0]
    layers, triple, width = in_t.shape
    heads = triple // 3 // HEAD_DIM
    embedded = dot("ipc,cd->ipd", images, patch_w)
    resid = jnp.concatenate([jnp.zeros((image_count, 1, width), FL), embedded], 1) + pos_t[None]
    tokens = resid.shape[1]
    saved = []
    for layer in range(layers):
        normed, unit_a, inv_a = layer_norm(resid, norm_t[4 * layer], norm_t[4 * layer + 1])
        rows_a = normed.astype(BF)
        joined = dot("itd,ed->ite", rows_a, in_t[layer]).astype(BF)
        joined = joined.reshape(image_count, tokens, 3, heads, HEAD_DIM)
        scores = dot("ithe,ishe->ihts", joined[:, :, 0], joined[:, :, 1]) * HEAD_DIM ** (-0.5)
        grown = jnp.exp(scores - jnp.max(scores, -1, keepdims=True))
        probs = grown / jnp.sum(grown, -1, keepdims=True)
        attended = dot("ihts,ishe->ithe", probs.astype(BF), joined[:, :, 2]).astype(BF)
        attended = attended.reshape(image_count, tokens, heads * HEAD_DIM)
        mid = resid + dot("ite,de->itd", attended, out_t[layer])
        normed, unit_b, inv_b = layer_norm(mid, norm_t[4 * layer + 2], norm_t[4 * layer + 3])
        rows_b = normed.astype(BF)
        pre = dot("itd,fd->itf", rows_b, up_t[layer])
        active = gelu(pre).astype(BF)
        resid = mid + dot("itf,fd->itd", active, down_t[layer])
        saved.append(
            (rows_a, unit_a, inv_a, joined, probs, attended, rows_b, unit_b, inv_b, pre, active)
        )
    normed, unit_f, inv_f = layer_norm(resid[:, 0], norm_t[4 * layers], norm_t[4 * layers + 1])
    features = normed.astype(BF)
    logits = dot("id,dc->ic", features, head_w)
    row_max = jnp.max(logits, -1, keepdims=True)
    log_total = row_max + jnp.log(jnp.sum(jnp.exp(logits - row_max), -1, keepdims=True))
    score = log_total[:, 0] - jnp.mean(logits, -1)
    loss = jnp.sum(counts * log_total[:, 0]) - jnp.sum(target_weight * logits)
    d_logits = (counts[:, None] * jnp.exp(logits - log_total) - target_weight).astype(BF)
    d_head = dot("id,ic->dc", features, d_logits)
    d_features = dot("ic,dc->id", d_logits, head_w)
    d_final, gain_f, bias_f = layer_norm_grad(d_features, unit_f, inv_f, norm_t[4 * layers])
    d_resid = jnp.zeros_like(resid).at[:, 0].set(d_final)
    d_mats = [None] * layers
    d_norm = [None] * (4 * layers) + [gain_f, bias_f]
    for layer in reversed(range(layers)):
        rows_a, unit_a, inv_a, joined, probs, attended, rows_b, unit_b, inv_b, pre, active = saved[
            layer
        ]
        upper = d_resid.astype(BF)
        d_down = dot("itf,itd->fd", active, upper)
        d_pre = (dot("itd,fd->itf", upper, down_t[layer]) * gelu_slope(pre)).astype(BF)
        d_up = dot("itf,itd->fd", d_pre, rows_b)
        d_rows = dot("itf,fd->itd", d_pre, up_t[layer])
        d_mid, d_norm[4 * layer + 2], d_norm[4 * layer + 3] = layer_norm_grad(
            d_rows, unit_b, inv_b, norm_t[4 * layer + 2]
        )
        d_mid = d_mid + d_resid
        upper = d_mid.astype(BF)
        d_out = dot("itd,ite->de", upper, attended)
        d_att = dot("itd,de->ite", upper, out_t[layer]).astype(BF)
        d_att = d_att.reshape(image_count, tokens, heads, HEAD_DIM)
        d_probs = dot("ithe,ishe->ihts", d_att, joined[:, :, 2])
        d_scores = (probs * (d_probs - jnp.sum(d_probs * probs, -1, keepdims=True))).astype(BF)
        d_value = dot("ihts,ithe->ishe", probs.astype(BF), d_att)
        d_query = dot("ihts,ishe->ithe", d_scores, joined[:, :, 1]) * HEAD_DIM ** (-0.5)
        d_keys = dot("ihts,ithe->ishe", d_scores, joined[:, :, 0]) * HEAD_DIM ** (-0.5)
        d_joined = jnp.stack([d_query, d_keys, d_value], 2).astype(BF)
        d_joined = d_joined.reshape(image_count, tokens, triple)
        d_in = dot("ite,itd->ed", d_joined, rows_a)
        d_rows = dot("ite,ed->itd", d_joined, in_t[layer])
        d_low, d_norm[4 * layer], d_norm[4 * layer + 1] = layer_norm_grad(
            d_rows, unit_a, inv_a, norm_t[4 * layer]
        )
        d_resid = d_mid + d_low
        d_mats[layer] = (d_in, d_out, d_up, d_down)
    d_patch = dot("ipc,ipd->cd", images, d_resid[:, 1:].astype(BF))
    d_pos = jnp.sum(d_resid, 0)
    return (loss, score, d_mats, d_patch, d_head, d_pos.T, jnp.stack(d_norm, 1))


def greet_column(k, c, z, y_peer, x_peer):
    barrier = pltpu.get_barrier_semaphore()

    def signal(dp, mp):
        pl.semaphore_signal(barrier, inc=1, device_id=(dp, mp), device_id_type=MESH)

    signal(k, 1 - c)
    for step in range(1, LINE):
        for core in range(2):
            signal(k - k % 4 + (k + step) % 4, core)
        signal(k % 4 + 4 * ((z + step) % LINE), c)
    pl.semaphore_wait(barrier, 3 * LINE - 2)


def landed(ref, sem):
    pltpu.make_async_copy(ref, ref, sem).wait()


def along(left, right, left_dim, right_dim):
    return lax.dot_general(
        left, right, (((left_dim,), (right_dim,)), ((), ())), preferred_element_type=FL
    )


def step_kernel(
    tokens,
    classes,
    image_ref,
    pick_rows_ref,
    pick_weight_ref,
    pick_label_ref,
    in_ref,
    out_ref,
    up_ref,
    down_ref,
    patch_ref,
    head_ref,
    pos_ref,
    norm_ref,
    own_ref,
    other_ref,
    stat_ref,
    score_ref,
    work,
    table,
    places,
    w_in,
    w_out,
    w_head,
    flat,
    resid,
    rows_a,
    unit_a,
    joined,
    probs,
    attended,
    rows_b,
    unit_b,
    inverses,
    active,
    slope,
    upper,
    final,
    d_norm,
    core_in,
    first_in,
    second_in,
    line_in,
    result,
    stats,
    stats_in,
    pack,
    fetch_line_sem,
    fetch_far_sem,
    fetch_near_sem,
    fetch_core_sem,
    fetch_own_sem,
    core_sem,
    first_sem,
    second_sem,
    line_sem,
    swap_sem,
    stat_sem,
):
    k, c, z, y, x, y_peer, x_peer = place()
    greet_column(k, c, z, y_peer, x_peer)
    image_count, padded, width = resid.shape
    dp_size = work.shape[1]
    n_in, n_out, n_up, n_down = [ref.shape[0] for ref in (in_ref, out_ref, up_ref, down_ref)]
    lead = n_in + n_out + n_up + n_down
    patch_rows = patch_ref.shape[0]
    head_rows = width // dp_size
    head_parts = w_head.shape[1] // width
    layers = 2
    rows_all = image_count * padded
    per = 2 * width // n_up
    wide = per * n_up
    share = SHARE
    first_step, second_step = 1 + c, 2 - c
    near = jnp.where(c == 0, x, y)
    far = jnp.where(c == 0, y, x)
    first_peer = (k + (1 - 2 * near) * first_step, c)
    second_peer = (k + (1 - 2 * far) * second_step, c)
    core, left, right = (k, 1 - c), (k - 4, c), (k + 4, c)

    def item(near_at, far_at):
        return near_at * first_step + far_at * second_step

    def job_layer(job):
        return 1 - job // 2

    def rows_of(job, of_core):
        start = share * (1 + of_core) if job % 2 == 0 else 3 * share * of_core
        return pl.ds(pl.multiple_of(start, 16), share)

    def dest(turn):
        early = jnp.where(turn == 0, 3 * (1 - z // 2), (2 + 3 * z) % 5)
        return jnp.where(turn < 2, early, jnp.where(turn == 2, 1 + z % 2, z))

    def remote(source, target, sems, index, peer):
        return pltpu.make_async_remote_copy(
            src_ref=source,
            dst_ref=target,
            send_sem=sems.at[(0,) + index],
            recv_sem=sems.at[(1,) + index],
            device_id=peer,
            device_id_type=MESH,
        )

    def to_core(job, d):
        group = pl.ds(pl.multiple_of(4 * d, 4), 4)
        return remote(
            work.at[job_layer(job), group, rows_of(job, 1 - c)],
            core_in.at[job, d],
            core_sem,
            (job, d),
            core,
        )

    def first_copy(job, d, far_at):
        return remote(
            core_in.at[job, d, item(1 - near, far_at)],
            first_in.at[job, d, far_at],
            first_sem,
            (job, d, far_at),
            first_peer,
        )

    def second_copy(job, d):
        return remote(
            core_in.at[job, d, item(near, 1 - far)],
            second_in.at[job, d],
            second_sem,
            (job, d),
            second_peer,
        )

    def line_copy(job, d, way):
        slot = d if way == 1 else jnp.where(d == z - 1, LINE, d)
        return remote(
            core_in.at[job, d, item(near, far)],
            line_in.at[job, slot],
            line_sem,
            (job, way, d),
            right if way == 1 else left,
        )

    def line_arrival(job, d, way):
        slot = d if way == 1 else jnp.where(d == z, LINE, d)
        landed(line_in.at[job, slot], line_sem.at[1, job, way, d])
        return line_in[job, slot].astype(FL)

    def part_of(job, d, q):
        block = work[job_layer(job), 4 * d + q, rows_of(job, c)].astype(FL)
        return block + core_in[job, d, q].astype(FL)

    def job_start(job):
        for turn in range(LINE):
            to_core(job, dest(turn)).start()

    def stage_core(job, d):
        landed(core_in.at[job, d], core_sem.at[1, job, d])
        for far_at in range(2):
            q = item(1 - near, far_at)
            core_in[job, d, q] = part_of(job, d, q).astype(BF)
            first_copy(job, d, far_at).start()

    def stage_first(job, d):
        for far_at in range(2):
            landed(first_in.at[job, d, far_at], first_sem.at[1, job, d, far_at])
        q = item(near, 1 - far)
        total = part_of(job, d, q) + first_in[job, d, 1 - far].astype(FL)
        core_in[job, d, q] = total.astype(BF)
        second_copy(job, d).start()

    def stage_second(job, d):
        landed(second_in.at[job, d], second_sem.at[1, job, d])
        q = item(near, far)
        result[job] = (
            part_of(job, d, q) + first_in[job, d, far].astype(FL) + second_in[job, d].astype(FL)
        )

        @pl.when(jnp.logical_and(d <= z, z < LINE - 1))
        def _():
            result[job] = result[job] + line_arrival(job, d, 0)

        @pl.when(jnp.logical_and(d >= z, z > 0))
        def _():
            result[job] = result[job] + line_arrival(job, d, 1)

        @pl.when(d != z)
        def _():
            core_in[job, d, q] = result[job].astype(BF)

        @pl.when(d < z)
        def _():
            line_copy(job, d, 0).start()

        @pl.when(d > z)
        def _():
            line_copy(job, d, 1).start()

    middle = jnp.minimum(z, 1) * jnp.minimum(LINE - 1 - z, 1)

    def serve(slot, jobs):
        for job in jobs:
            age = slot - JOB_SLOTS[job]
            due(age, stage_core, job)
            due(age - 2, stage_first, job)
            due(age - 5 - middle, stage_second, job)

    def serve_static(job, turn):
        if turn < LINE:
            stage_core(job, dest(turn))
        if 1 <= turn < LINE + 1:
            stage_first(job, dest(turn - 1))
        if turn >= 2:
            stage_second(job, dest(turn - 2))

    def swap(job):
        rows = rows_of(job, c)
        return remote(result.at[job], own_ref.at[rows], swap_sem, (job,), core)

    def job_finish(job):
        layer = job_layer(job)

        @pl.when(c == layer)
        def _():
            own_ref[rows_of(job, c)] = result[job]

        @pl.when(c != layer)
        def _():
            swap(job).start()

    def job_close(job):
        for turn in range(LINE):
            d = dest(turn)
            to_core(job, d).wait_send()
            first_copy(job, d, 0).wait_send()
            first_copy(job, d, 1).wait_send()
            second_copy(job, d).wait_send()

            @pl.when(d < z)
            def _():
                line_copy(job, d, 0).wait_send()

            @pl.when(d > z)
            def _():
                line_copy(job, d, 1).wait_send()

    edge = 1 - middle

    def fetch_rows(job, of_core):
        start = share * (1 + of_core) if job % 2 == 1 else 3 * share * of_core
        return pl.ds(pl.multiple_of(start, 16), share)

    def fetch_copy(job, d, q, sems, index, peer):
        block = work.at[job // 2, 4 * d + q, fetch_rows(job, c)]
        return remote(block, block, sems, (job,) + index, peer)

    def fetch_line(job, d, way):
        peer = right if way == 1 else left
        return fetch_copy(job, d, item(near, far), fetch_line_sem, (way, d), peer)

    def fetch_far(job, d):
        return fetch_copy(job, d, item(near, far), fetch_far_sem, (d,), second_peer)

    def fetch_near(job, d, which):
        q = item(near, far if which == 0 else 1 - far)
        return fetch_copy(job, d, q, fetch_near_sem, (d, which), first_peer)

    def fetch_group(job, d, of_core):
        group = pl.ds(pl.multiple_of(4 * d, 4), 4)
        return work.at[job // 2, group, fetch_rows(job, of_core)]

    def fetch_core(job, d):
        block = fetch_group(job, d, c)
        return remote(block, block, fetch_core_sem, (job, d), core)

    def fetch_own(job):
        source = pack.at[pl.ds(0 if job == 1 else share * (job - 2), share)]
        rows = fetch_rows(job, 1 - c)
        return remote(source, work.at[job // 2, k, rows], fetch_own_sem, (job,), core)

    def block_landed(job, d, q, sem):
        landed(work.at[job // 2, 4 * d + q, fetch_rows(job, c)], sem)

    def fetch_begin(job):
        if job == 1:

            @pl.when(c == 1)
            def _():
                landed(work.at[0, k, fetch_rows(job, c)], fetch_own_sem.at[1, job])

        if job >= 2:

            @pl.when(c == 0)
            def _():
                landed(work.at[1, k, fetch_rows(job, c)], fetch_own_sem.at[1, job])

        @pl.when(z < LINE - 1)
        def _():
            fetch_line(job, z, 1).start()

        @pl.when(z > 0)
        def _():
            fetch_line(job, z, 0).start()

        fetch_far(job, z).start()
        fetch_near(job, z, 0).start()

    def stage_line(job, d):
        @pl.when(d < z)
        def _():
            block_landed(job, d, item(near, far), fetch_line_sem.at[1, job, 1, d])

            @pl.when(z < LINE - 1)
            def _():
                fetch_line(job, d, 1).start()

        @pl.when(d > z)
        def _():
            block_landed(job, d, item(near, far), fetch_line_sem.at[1, job, 0, d])

            @pl.when(z > 0)
            def _():
                fetch_line(job, d, 0).start()

        @pl.when(d != z)
        def _():
            fetch_far(job, d).start()
            fetch_near(job, d, 0).start()

    def stage_far(job, d):
        block_landed(job, d, item(near, 1 - far), fetch_far_sem.at[1, job, d])
        fetch_near(job, d, 1).start()

    def stage_near(job, d):
        block_landed(job, d, item(1 - near, far), fetch_near_sem.at[1, job, d, 0])
        block_landed(job, d, item(1 - near, 1 - far), fetch_near_sem.at[1, job, d, 1])
        fetch_core(job, d).start()

    def due(age, stage, job, nearest_first=False):
        def act(turn):
            stage(job, dest(LINE - 1 - turn if nearest_first else turn))

        if isinstance(age, int):
            if age % 2 == 0 and 0 <= age < 2 * LINE:
                act(age // 2)
            return

        @pl.when(jnp.logical_and(age % 2 == 0, jnp.logical_and(age >= 0, age < 2 * LINE)))
        def _():
            act(age // 2)

    def fetch(slot, jobs):
        for job in jobs:
            age = slot - FETCH_SLOTS[job]
            if isinstance(age, int):
                if age == 0:
                    fetch_begin(job)
            else:

                @pl.when(age == 0)
                def _():
                    fetch_begin(job)

            due(age - edge, stage_line, job, True)
            due(age - 2 - edge, stage_far, job, True)
            due(age - 4 - edge, stage_near, job, True)

    def fetch_ready(job):
        for d in range(LINE):
            landed(fetch_group(job, d, 1 - c), fetch_core_sem.at[1, job, d])

    def fetch_close():
        for job in range(4):
            for d in range(LINE):
                fetch_far(job, d).wait_send()
                fetch_near(job, d, 0).wait_send()
                fetch_near(job, d, 1).wait_send()
                fetch_core(job, d).wait_send()

                @pl.when(jnp.logical_and(d <= z, z < LINE - 1))
                def _():
                    fetch_line(job, d, 1).wait_send()

                @pl.when(jnp.logical_and(d >= z, z > 0))
                def _():
                    fetch_line(job, d, 0).wait_send()

        @pl.when(c == 0)
        def _():
            fetch_own(1).wait_send()

        @pl.when(c == 1)
        def _():
            fetch_own(2).wait_send()
            fetch_own(3).wait_send()

    def attention_shard():
        return jnp.concatenate([in_ref[...], out_ref[...]], 0).astype(BF)

    @pl.when(c == 0)
    def _():
        work[0, k, 0:share] = attention_shard()
        work[0, k, share : 2 * share] = up_ref[...].astype(BF)
        pack[0:share] = down_ref[...].astype(BF)

    @pl.when(c == 1)
    def _():
        flat[0:512] = jnp.zeros((512, width), FL)
        flat[0 : norm_ref.shape[0], 0:head_rows] = norm_ref[...]
        flat[128 : 128 + head_rows, 0:tokens] = pos_ref[...]
        flat[128 : 128 + head_rows, tokens : tokens + norm_ref.shape[0]] = flat[0:128, 0:128].T[
            0:head_rows, 0 : norm_ref.shape[0]
        ]
        exact = flat[128 : 128 + head_rows]
        high = exact.astype(BF).astype(FL)
        tail = jnp.concatenate([patch_ref[...], high, exact - high], 0)
        work[0, k, lead:] = tail.astype(BF)
        for part in range(head_parts):
            stop = min(classes, (part + 1) * width)
            rows = slice(256 + part * head_rows, 256 + (part + 1) * head_rows)
            flat[rows, 0 : stop - part * width] = head_ref[:, part * width : stop]
        work[1, k, lead:] = flat[256 : 256 + share].astype(BF)
        work[1, k, 2 * share : 3 * share] = down_ref[...].astype(BF)
        pack[0:share] = attention_shard()
        pack[share : 2 * share] = up_ref[...].astype(BF)

    for slot in range(12):
        fetch(slot, (0, 1))
        if slot == 0:

            @pl.when(c == 0)
            def _():
                fetch_own(1).start()

            @pl.when(c == 1)
            def _():
                fetch_own(2).start()
                fetch_own(3).start()

    fetch_ready(0)

    def spread_table(i, carry):
        block = work[0, i, lead + patch_rows :].astype(FL)
        flat[pl.ds(pl.multiple_of(i * head_rows, 8), head_rows)] = (
            block[:head_rows] + block[head_rows:]
        )
        return carry

    lax.fori_loop(0, dp_size, spread_table, 0)
    table[...] = flat[0:width, 0 : table.shape[0]].T
    places[...] = jnp.zeros_like(places)
    places[0 : tokens - 1] = table[1:tokens]
    places[tokens - 1 : tokens] = table[0:1]

    def norm_row(column):
        return table[tokens + column : tokens + column + 1]

    def spread_mats(layer):
        def take(k, carry):
            block = work[layer, k, 0 : n_in + n_out].astype(FL)
            flat[pl.ds(pl.multiple_of(k * n_in, 8), n_in)] = block[:n_in]
            flat[pl.ds(pl.multiple_of(dp_size * n_in + k * n_out, 8), n_out)] = block[n_in:]
            return carry

        lax.fori_loop(0, dp_size, take, 0)
        w_in[layer] = flat[0 : dp_size * n_in].astype(BF)
        w_out[layer] = flat[dp_size * n_in :].astype(BF)

    def up_part(layer, part):
        return work[layer, part * per : (part + 1) * per, n_in + n_out : lead - n_down].reshape(
            wide, width
        )

    def down_part(layer, part):
        return work[layer, part * per : (part + 1) * per, lead - n_down : lead].reshape(
            wide, width
        )

    parts = dp_size // per
    lane = lax.broadcasted_iota(jnp.int32, (1, 128), 1)
    low_lanes = lane < HEAD_DIM
    low_one = low_lanes.astype(FL).astype(BF)
    high_one = (1.0 - low_lanes.astype(FL)).astype(BF)
    scale = HEAD_DIM ** (-0.5)
    low_scaled = (low_lanes.astype(FL) * scale).astype(BF)
    high_scaled = ((1.0 - low_lanes.astype(FL)) * scale).astype(BF)
    real_key = lax.broadcasted_iota(jnp.int32, (2 * padded, padded), 1) < tokens
    pairs = width // 128

    def both_heads(values, low, high):
        return jnp.concatenate([values * low, values * high], 0)

    def one_head(values):
        return jnp.where(low_lanes, values[:padded], values[padded:])

    patch_w = work[0, :, lead : lead + patch_rows].reshape(dp_size * patch_rows, width)

    def embed(i, carry):
        resid[i] = jnp.dot(image_ref[i], patch_w, preferred_element_type=FL) + places[...]
        return carry

    lax.fori_loop(0, image_count, embed, 0)

    for layer in range(layers):
        if layer > 0:
            fetch_ready(2 * layer)
        spread_mats(layer)
        gain_a, bias_a, gain_b, bias_b = [norm_row(4 * layer + column) for column in range(4)]

        def forward(i, carry):
            values = resid[i]
            normed, unit, inverse = layer_norm(values, gain_a, bias_a)
            unit_a[layer, i] = unit.astype(BF)
            inverses[layer, i, :, 0:1] = inverse
            normed = normed.astype(BF)
            rows_a[layer, i] = normed
            joined[layer, i] = along(normed, w_in[layer], 1, 1).astype(BF)
            for pair in range(pairs):
                at = 128 * pair
                query = both_heads(
                    joined[layer, i, :, at : at + 128], low_scaled, high_scaled
                )
                keys = joined[layer, i, :, width + at : width + at + 128]
                value = joined[layer, i, :, 2 * width + at : 2 * width + at + 128]
                scores = jnp.where(real_key, along(query, keys, 1, 1), -1e30)
                grown = jnp.exp(scores - jnp.max(scores, -1, keepdims=True))
                prob = (grown * (1.0 / jnp.sum(grown, -1, keepdims=True))).astype(BF)
                probs[layer, i, pair] = prob
                mixed = one_head(jnp.dot(prob, value, preferred_element_type=FL))
                attended[layer, i, :, at : at + 128] = mixed.astype(BF)
                if pair == 1:
                    fetch(12 + 16 * layer + 2 * i, (1, 2) if layer == 0 else (3,))
            resid[i] = values + along(attended[layer, i], w_out[layer], 1, 1)
            fetch(13 + 16 * layer + 2 * i, (1, 2) if layer == 0 else (3,))
            return carry

        lax.fori_loop(0, image_count, forward, 0)
        fetch_ready(2 * layer + 1)

        def forward_mlp(i, carry):
            mid = resid[i]
            normed, unit, inverse = layer_norm(mid, gain_b, bias_b)
            unit_b[layer, i] = unit.astype(BF)
            inverses[layer, i, :, 1:2] = inverse
            normed = normed.astype(BF)
            rows_b[layer, i] = normed
            for part in range(parts):
                pre = along(normed, up_part(layer, part), 1, 1)
                phi = 0.5 + 0.5 * lax.erf(pre * math.sqrt(0.5))
                bell = math.sqrt(0.5 / math.pi) * jnp.exp(-0.5 * pre * pre)
                act = (pre * phi).astype(BF)
                lanes = slice(part * wide, (part + 1) * wide)
                active[layer, i, :, lanes] = act
                slope[layer, i, :, lanes] = (phi + pre * bell).astype(BF)
                mid = mid + jnp.dot(act, down_part(layer, part), preferred_element_type=FL)
                if layer == 0:
                    fetch(20 + 2 * i + part, (2, 3))
            resid[i] = mid
            return carry

        lax.fori_loop(0, image_count, forward_mlp, 0)

    fetch_close()

    def spread_head(k, carry):
        block = work[1, k, lead:].astype(FL)
        for part in range(head_parts):
            flat[
                pl.ds(pl.multiple_of(part * width + k * head_rows, 8), head_rows)
            ] = block[part * head_rows : (part + 1) * head_rows]
        return carry

    lax.fori_loop(0, dp_size, spread_head, 0)
    for part in range(head_parts):
        w_head[:, part * width : (part + 1) * width] = flat[
            part * width : (part + 1) * width
        ].astype(BF)

    final[...] = jnp.zeros_like(final)
    for i in range(image_count):
        final[i : i + 1] = resid[i, tokens - 1 : tokens]
    gain_f, bias_f = norm_row(4 * layers), norm_row(4 * layers + 1)
    normed, unit, inverse = layer_norm(final[...], gain_f, bias_f)
    features = normed.astype(BF)
    logits = jnp.dot(features, w_head[...], preferred_element_type=FL)
    real = lax.broadcasted_iota(jnp.int32, logits.shape, 1) < classes
    row_max = jnp.max(jnp.where(real, logits, -1e30), -1, keepdims=True)
    grown = jnp.where(real, jnp.exp(logits - row_max), 0.0)
    total = jnp.sum(grown, -1, keepdims=True)
    log_total = row_max + jnp.log(total)
    row = lax.broadcasted_iota(jnp.int32, logits.shape, 0)
    column = lax.broadcasted_iota(jnp.int32, logits.shape, 1)
    count = jnp.zeros((logits.shape[0], 1), FL)
    target = jnp.zeros_like(logits)
    for pick in range(pick_rows_ref.shape[0]):
        chosen = row == pick_rows_ref[pick] - c * image_count
        weight = pick_weight_ref[pick].astype(FL)
        count = count + jnp.where(chosen[:, 0:1], weight, 0.0)
        hit = jnp.logical_and(chosen, column == pick_label_ref[pick])
        target = target + jnp.where(hit, weight, 0.0)
    image_row = row[:, 0:1] < image_count
    count = jnp.where(image_row, count, 0.0)
    target = jnp.where(image_row, target, 0.0)
    mean = jnp.sum(jnp.where(real, logits, 0.0), -1, keepdims=True) / classes
    score_ref[...] = jnp.broadcast_to(log_total - mean, score_ref.shape)
    loss = jnp.sum(count * log_total, keepdims=True) - jnp.sum(target * logits, keepdims=True)
    row = lax.broadcasted_iota(jnp.int32, (8, 128), 0)
    column = lax.broadcasted_iota(jnp.int32, (8, 128), 1)
    stat = jnp.where(row == 0, loss, jnp.where(row == 1, jnp.sum(count, keepdims=True), 0.0))
    stats[0, 0:8] = jnp.where(column == 0, stat, 0.0)
    d_logits = (count * (grown / total) - target).astype(BF)
    d_head = along(features, d_logits, 0, 0)
    for part in range(head_parts):
        flat[part * width : (part + 1) * width] = d_head[:, part * width : (part + 1) * width]

    def pack_head(k, carry):
        blocks = [
            flat[pl.ds(pl.multiple_of(part * width + k * head_rows, 8), head_rows)]
            for part in range(head_parts)
        ]
        blocks.append(jnp.zeros((work.shape[2] - lead - head_parts * head_rows, width), FL))
        work[1, k, lead:] = jnp.concatenate(blocks, 0).astype(BF)
        return carry

    lax.fori_loop(0, dp_size, pack_head, 0)
    d_features = along(d_logits, w_head[...], 1, 1)
    d_norm[...] = jnp.zeros_like(d_norm)

    def norm_back(upstream, unit, inverse, gain, column):
        unit = unit.astype(FL)
        row = slice(column, column + 1)
        d_norm[row] = d_norm[row] + jnp.sum(upstream * unit, 0, keepdims=True)
        row = slice(column + 1, column + 2)
        d_norm[row] = d_norm[row] + jnp.sum(upstream, 0, keepdims=True)
        scaled = upstream * gain
        return inverse * (
            scaled
            - jnp.mean(scaled, -1, keepdims=True)
            - unit * jnp.mean(scaled * unit, -1, keepdims=True)
        )

    final[...] = norm_back(d_features, unit, inverse, gain_f, 4 * layers)
    resid[...] = jnp.zeros_like(resid)
    for i in range(image_count):
        resid[i, tokens - 1 : tokens] = final[i : i + 1]

    def all_rows(ref, *spot):
        return ref[spot].reshape(rows_all, -1)

    every = slice(None)
    for layer in reversed(range(layers)):
        gain_a, gain_b = norm_row(4 * layer), norm_row(4 * layer + 2)

        def back_mlp(i, carry):
            grad = resid[i]
            low = grad.astype(BF)
            upper[i] = low
            d_rows = jnp.zeros((padded, width), FL)
            for part in range(parts):
                lanes = slice(part * wide, (part + 1) * wide)
                d_pre = along(low, down_part(layer, part), 1, 1) * slope[
                    layer, i, :, lanes
                ].astype(FL)
                d_pre = d_pre.astype(BF)
                slope[layer, i, :, lanes] = d_pre
                d_rows = d_rows + jnp.dot(
                    d_pre, up_part(layer, part), preferred_element_type=FL
                )
            if layer < layers - 1:
                serve(10 + i, (0, 1))
            resid[i] = grad + norm_back(
                d_rows, unit_b[layer, i], inverses[layer, i, :, 1:2], gain_b, 4 * layer + 2
            )
            return carry

        lax.fori_loop(0, image_count, back_mlp, 0)
        if layer < layers - 1:
            job_finish(0)
        few = per // 2
        for part in range(2 * parts):
            lanes = slice(part * width, (part + 1) * width)
            spot = slice(part * few, (part + 1) * few)
            grad = along(
                all_rows(active, layer, every, every, lanes), all_rows(upper, every), 0, 0
            )
            work[layer, spot, lead - n_down : lead] = grad.astype(BF).reshape(
                few, n_down, width
            )
            grad = along(
                all_rows(slope, layer, every, every, lanes), all_rows(rows_b, layer), 0, 0
            )
            work[layer, spot, n_in + n_out : lead - n_down] = grad.astype(BF).reshape(
                few, n_up, width
            )
            if layer < layers - 1:
                serve(14 + part, (1,))

        job = 2 * (layers - 1 - layer)
        job_start(job)
        first_slot = 18 * (layers - 1 - layer)
        jobs = (0,) if layer == layers - 1 else (1, 2)

        def back_attention(i, carry):
            grad = resid[i]
            low = grad.astype(BF)
            upper[i] = low
            d_att = jnp.dot(low, w_out[layer], preferred_element_type=FL).astype(BF)
            for pair in range(pairs):
                at = 128 * pair
                query = both_heads(
                    joined[layer, i, :, at : at + 128], low_scaled, high_scaled
                )
                keys = joined[layer, i, :, width + at : width + at + 128]
                value = joined[layer, i, :, 2 * width + at : 2 * width + at + 128]
                prob = probs[layer, i, pair]
                d_pair = both_heads(d_att[:, at : at + 128], low_one, high_one)
                d_probs = along(d_pair, value, 1, 1)
                wide = prob.astype(FL)
                moved = wide * d_probs
                d_scores = (moved - wide * jnp.sum(moved, -1, keepdims=True)).astype(BF)
                d_query = one_head(jnp.dot(d_scores, keys, preferred_element_type=FL)) * scale
                d_keys = along(d_scores, query, 0, 0)
                d_value = along(prob, d_pair, 0, 0)
                active[layer, i, :, at : at + 128] = d_query.astype(BF)
                active[layer, i, :, width + at : width + at + 128] = d_keys.astype(BF)
                active[layer, i, :, 2 * width + at : 2 * width + at + 128] = d_value.astype(BF)
                if pair == 1:
                    serve(first_slot + 2 * i, jobs)
            d_rows = jnp.dot(
                active[layer, i, :, 0 : 3 * width], w_in[layer], preferred_element_type=FL
            )
            serve(first_slot + 2 * i + 1, jobs)
            resid[i] = grad + norm_back(
                d_rows, unit_a[layer, i], inverses[layer, i, :, 0:1], gain_a, 4 * layer
            )
            return carry

        lax.fori_loop(0, image_count, back_attention, 0)
        if layer < layers - 1:
            job_finish(1)
        for part in range(3):
            lanes = slice(part * width, (part + 1) * width)
            flat[lanes] = along(
                all_rows(active, layer, every, every, lanes), all_rows(rows_a, layer), 0, 0
            )
            if part > 0:
                serve(first_slot + 7 + part, jobs[-1:])
        flat[3 * width :] = along(all_rows(upper, every), all_rows(attended, layer), 0, 0)

        def pack_mats(k, carry):
            block = jnp.concatenate(
                [
                    flat[pl.ds(pl.multiple_of(k * n_in, 8), n_in)],
                    flat[pl.ds(pl.multiple_of(dp_size * n_in + k * n_out, 8), n_out)],
                ],
                0,
            )
            work[layer, k, 0 : n_in + n_out] = block.astype(BF)
            return carry

        lax.fori_loop(0, dp_size, pack_mats, 0)
        if layer > 0:
            job_start(1)

    places[...] = jnp.zeros_like(places)

    def last(i, carry):
        grad = resid[i]
        upper[i] = grad.astype(BF)
        places[...] = places[...] + grad
        return carry

    lax.fori_loop(0, image_count, last, 0)
    per_patch = width // patch_rows
    for part in range(dp_size // per_patch):
        lanes = slice(part * width, (part + 1) * width)
        grad = along(
            image_ref[:, :, lanes].reshape(rows_all, width), all_rows(upper, every), 0, 0
        )
        work[0, part * per_patch : (part + 1) * per_patch, lead : lead + patch_rows] = grad.astype(
            BF
        ).reshape(per_patch, patch_rows, width)
        serve(28 + part, (2,))
    table[...] = jnp.zeros_like(table)
    table[0:1] = places[tokens - 1 : tokens]
    table[1:tokens] = places[0 : tokens - 1]
    table[tokens : tokens + 4 * layers + 2] = d_norm[0 : 4 * layers + 2]
    flat[0:width] = jnp.zeros((width, width), FL)
    flat[0:width, 0 : table.shape[0]] = table[...].T

    def pack_table(k, carry):
        block = flat[pl.ds(pl.multiple_of(k * head_rows, 8), head_rows)]
        rest = jnp.zeros((work.shape[2] - lead - patch_rows - head_rows, width), FL)
        work[0, k, lead + patch_rows :] = jnp.concatenate([block, rest], 0).astype(BF)
        return carry

    lax.fori_loop(0, dp_size, pack_table, 0)
    serve(30, (2,))
    job_start(3)
    job_finish(2)
    for turn in range(LINE + 2):
        serve_static(3, turn)
    job_finish(3)

    def small_copy():
        return remote(result.at[1], other_ref, swap_sem, (4,), core)

    @pl.when(c == 1)
    def _():
        small_copy().start()
        other_ref[...] = result[3]

    squares = jnp.zeros((8, width), FL)
    for job in range(4):

        def add(i, total, job=job):
            rows = result[job, pl.ds(pl.multiple_of(i * 8, 8), 8)]
            return total + rows * rows

        squares = lax.fori_loop(0, share // 8, add, squares, unroll=4)
    stats[0, 8:16] = squares[:, 0:128] + squares[:, 128:256] + squares[:, 256:384]

    def stat_copy(slot, step, peer):
        return pltpu.make_async_remote_copy(
            src_ref=stats.at[0] if slot < 8 else stats.at[1],
            dst_ref=stats_in.at[2 * (k % 4) + c] if slot < 8 else stats_in.at[8 + z],
            send_sem=stat_sem.at[0, step],
            recv_sem=stat_sem.at[1, 2 * (k % 4) + c] if slot < 8 else stat_sem.at[1, 8 + z],
            device_id=peer,
            device_id_type=MESH,
        )

    def plane_copy(step):
        place_of = (2 * (k % 4) + c + step) % 8
        return stat_copy(0, step, (k - k % 4 + place_of // 2, place_of % 2))

    def column_copy(step):
        return stat_copy(8, 8 + step, (k % 4 + 4 * ((z + step) % LINE), c))

    for step in range(1, 8):
        plane_copy(step).start()
    stats_in[2 * (k % 4) + c] = stats[0]
    for step in range(1, 8):
        source = (2 * (k % 4) + c + step) % 8
        landed(stats_in.at[source], stat_sem.at[1, source])
    total = stats_in[0]
    for source in range(1, 8):
        total = total + stats_in[source]
    stats[1] = total
    for step in range(1, LINE):
        column_copy(step).start()
    stats_in[8 + z] = total
    for step in range(1, LINE):
        source = 8 + (z + step) % LINE
        landed(stats_in.at[source], stat_sem.at[1, source])
    stat_ref[...] = (stats_in[8] + stats_in[9]) + (stats_in[10] + stats_in[11])

    for job in range(4):

        @pl.when(c != job_layer(job))
        def _():
            swap(job).wait_send()

        @pl.when(c == job_layer(job))
        def _():
            landed(own_ref.at[rows_of(job, 1 - c)], swap_sem.at[1, job])

        job_close(job)

    @pl.when(c == 1)
    def _():
        small_copy().wait_send()

    @pl.when(c == 0)
    def _():
        landed(other_ref, swap_sem.at[1, 4])

    for step in range(1, 8):
        plane_copy(step).wait_send()
    for step in range(1, LINE):
        column_copy(step).wait_send()


def whole_step(images, picks, mats, smalls):
    image_count, padded, patch_width = images.shape
    dp_size = lax.axis_size("dp")
    width = mats[0].shape[1]
    classes, tokens = smalls[1].shape[1], smalls[2].shape[1]
    head_width = -(-classes // width) * width
    in_vmem = pl.BlockSpec(memory_space=pltpu.VMEM)
    in_smem = pl.BlockSpec(memory_space=pltpu.SMEM)
    share = mats[2].shape[0]
    hidden = dp_size * share
    saved = (2, image_count, padded)
    here = (image_count, padded)
    rows = 4 * share
    own, other, stat, score = pl.pallas_call(
        lambda *refs: step_kernel(tokens, classes, *refs),
        out_shape=(
            jax.ShapeDtypeStruct((rows, width), FL),
            jax.ShapeDtypeStruct((share, width), FL),
            jax.ShapeDtypeStruct((16, 128), FL),
            jax.ShapeDtypeStruct((16, 128), FL),
        ),
        in_specs=[in_vmem] + [in_smem] * 3 + [in_vmem] * 8,
        out_specs=(in_vmem, in_vmem, in_vmem, in_vmem),
        scratch_shapes=[
            pltpu.VMEM((2, dp_size, rows, width), BF),
            pltpu.VMEM((256, width), FL),
            pltpu.VMEM((padded, width), FL),
            pltpu.VMEM((2, 3 * width, width), BF),
            pltpu.VMEM((2, width, width), BF),
            pltpu.VMEM((width, head_width), BF),
            pltpu.VMEM((4 * width, width), FL),
            pltpu.VMEM(here + (width,), FL),
            pltpu.VMEM(saved + (width,), BF),
            pltpu.VMEM(saved + (width,), BF),
            pltpu.VMEM(saved + (3 * width,), BF),
            pltpu.VMEM((2, image_count, width // 128, 2 * padded, padded), BF),
            pltpu.VMEM(saved + (width,), BF),
            pltpu.VMEM(saved + (width,), BF),
            pltpu.VMEM(saved + (width,), BF),
            pltpu.VMEM(saved + (2,), FL),
            pltpu.VMEM(saved + (hidden,), BF),
            pltpu.VMEM(saved + (hidden,), BF),
            pltpu.VMEM(here + (width,), BF),
            pltpu.VMEM((16, width), FL),
            pltpu.VMEM((16, width), FL),
            pltpu.VMEM((4, LINE, 4, share, width), BF),
            pltpu.VMEM((4, LINE, 2, share, width), BF),
            pltpu.VMEM((4, LINE, share, width), BF),
            pltpu.VMEM((4, LINE + 1, share, width), BF),
            pltpu.VMEM((4, share, width), FL),
            pltpu.VMEM((2, 16, 128), FL),
            pltpu.VMEM((8 + LINE, 16, 128), FL),
            pltpu.VMEM((2 * share, width), BF),
            pltpu.SemaphoreType.DMA((2, 4, 2, LINE)),
            pltpu.SemaphoreType.DMA((2, 4, LINE)),
            pltpu.SemaphoreType.DMA((2, 4, LINE, 2)),
            pltpu.SemaphoreType.DMA((2, 4, LINE)),
            pltpu.SemaphoreType.DMA((2, 4)),
            pltpu.SemaphoreType.DMA((2, 4, LINE)),
            pltpu.SemaphoreType.DMA((2, 4, LINE, 2)),
            pltpu.SemaphoreType.DMA((2, 4, LINE)),
            pltpu.SemaphoreType.DMA((2, 4, 2, LINE)),
            pltpu.SemaphoreType.DMA((2, 5)),
            pltpu.SemaphoreType.DMA((2, 8 + LINE)),
        ],
        compiler_params=pltpu.CompilerParams(
            collective_id=1, has_side_effects=True, vmem_limit_bytes=63 * 2**20
        ),
        name="forward_backward",
    )(images, *picks, *mats, *smalls)
    return (own, other, stat, score[:image_count, 0])


def pack_gradients(d_mats, d_patch, d_head, d_pos, d_norm, small_rows):
    dp_size = lax.axis_size("dp")
    width = d_patch.shape[1]
    classes = d_head.shape[1]
    head_rows, head_parts = d_head.shape[0] // dp_size, -(-classes // width)
    patch_rows = d_patch.shape[0] // dp_size
    head = jnp.pad(d_head, ((0, 0), (0, head_parts * width - classes)))
    head = head.reshape(dp_size, head_rows, head_parts, width).swapaxes(1, 2)
    head = head.reshape(dp_size, head_parts * head_rows, width)
    other = jnp.concatenate([d_pos, d_norm], 1)
    other = jnp.pad(other, ((0, 0), (0, width - other.shape[1])))
    other = other.reshape(dp_size, head_rows, width)
    tails = ([d_patch.reshape(dp_size, patch_rows, width), other], [head])
    layers = []
    for mats, tail in zip(d_mats, tails):
        chunks = [mat.reshape(dp_size, -1, width) for mat in mats] + tail
        rows = sum([chunk.shape[1] for chunk in chunks])
        lead = rows - sum([part.shape[1] for part in tail])
        total = lead + small_rows + 8
        chunks.append(jnp.zeros((dp_size, total - rows, width), FL))
        layers.append(jnp.concatenate(chunks, 1).astype(BF))
    return jnp.stack(layers)


def reduce_gradients(parts, small_rows, stat):
    own = lax.psum_scatter(parts.astype(FL), "mp", scatter_dimension=0, tiled=False)
    own = lax.psum_scatter(own, "dp", scatter_dimension=0, tiled=False)
    squares = jnp.zeros((8, 128), FL).at[0, 0].set(jnp.sum(own * own))
    stat = lax.psum(jnp.concatenate([stat, squares], 0), ("dp", "mp"))
    at = own.shape[0] - 8 - small_rows
    other = lax.ppermute(own[at : at + small_rows], "mp", ((0, 1), (1, 0)))
    return (own, other, stat)


def split(values):
    high = values.astype(BF)
    return (high, (values - high.astype(FL)).astype(BF))


def product(left, right):
    left_high, left_low = split(left)
    right_high, right_low = split(right)
    return jnp.dot(
        jnp.concatenate([left_high, left_high, left_low], 1),
        jnp.concatenate([right_high, right_low, right_high], 0),
        preferred_element_type=FL,
    )


def clip_scale(stat):
    weight_total = jnp.sum(stat[1:2], keepdims=True)
    grad_norm = jnp.sqrt(jnp.sum(stat[8:16], keepdims=True)) / weight_total
    scaling = THRESHOLD / jnp.maximum(grad_norm, THRESHOLD) / weight_total
    return (weight_total, grad_norm, scaling)


def new_moment(index, counts, own_ref, scaling, moment_ref, padded):
    count = counts[index]
    at = sum(counts[:index])
    moment = MOMENTUM * moment_ref[...] + own_ref[at : at + count] * scaling
    padded[0:count] = moment
    padded[count:] = jnp.zeros((padded.shape[0] - count, padded.shape[1]), FL)
    return moment


def gram_pack(padded, ref, index):
    moment = padded[...]
    high, low = split(moment.T)
    left = jnp.concatenate([high, high, low], 1)
    high, low = split(moment)
    right = jnp.concatenate([high, low, high], 0)
    at = 0
    for row in range(0, left.shape[0], 128):
        part = jnp.dot(left[row : row + 128], right[:, row:], preferred_element_type=FL)
        ref[index + (slice(None), slice(at, at + part.shape[1]))] = part
        at += part.shape[1]


def tri_pack(ref, index, whole):
    ref[index + (slice(None), slice(0, 384))] = whole[0:128]
    ref[index + (slice(None), slice(384, 640))] = whole[128:256, 128:384]
    ref[index + (slice(None), slice(640, 768))] = whole[256:384, 256:384]


def tri_unpack(tri, square):
    square[0:128, :] = tri[:, 0:384]
    square[128:256, 128:384] = tri[:, 384:640]
    square[256:384, 256:384] = tri[:, 640:768]
    square[128:256, 0:128] = tri[:, 128:256].T
    square[256:384, 0:128] = tri[:, 256:384].T
    square[256:384, 128:256] = tri[:, 512:640].T


def newton_schulz(square_ref):
    row = lax.broadcasted_iota(jnp.int32, square_ref.shape, 0)
    column = lax.broadcasted_iota(jnp.int32, square_ref.shape, 1)
    unit = (row == column).astype(FL)
    gram = square_ref[...]
    size = jnp.sqrt(jnp.sum(gram * unit, keepdims=True)) + 1e-07
    square_ref[...] = gram / (size * size)
    factor = None
    for turn in range(5):
        square = square_ref[...]
        mixed = NS_A * unit + NS_B * square + NS_C * product(square, square)
        factor = mixed if factor is None else product(mixed, factor)
        if turn < 4:
            square_ref[...] = product(product(mixed, square), mixed)
    return factor / size


def muon_kernel(
    own_ref,
    stat_ref,
    in_ref,
    out_ref,
    up_ref,
    down_ref,
    factor_ref,
    padded,
    tri,
    first_in,
    second_in,
    total,
    left_in,
    right_in,
    to_left_buf,
    to_right_buf,
    square,
    first_sem,
    second_sem,
    line_sem,
    spread_sem,
):
    k, c, z, y, x, y_peer, x_peer = place()
    greet(k, c, z, y_peer, x_peer)
    left, right = (k - 4, c), (k + 4, c)
    at_x, at_y = (x_peer, c), (y_peer, c)
    moments = (in_ref, out_ref, up_ref, down_ref)
    counts = [ref.shape[0] for ref in moments]
    part_a, part_b = pl.ds(0, 64), pl.ds(64, 64)

    def remote(source, target, sems, index, peer):
        return pltpu.make_async_remote_copy(
            src_ref=source,
            dst_ref=target,
            send_sem=sems.at[(0,) + index],
            recv_sem=sems.at[(1,) + index],
            device_id=peer,
            device_id_type=MESH,
        )

    scaling = clip_scale(stat_ref[...])[2]
    for index in range(4):
        new_moment(index, counts, own_ref, scaling, moments[index], padded)
        gram_pack(padded, tri, (index // 2, index % 2))

    chunks = (pl.ds(0, 32), pl.ds(64, 32), pl.ds(32, 32), pl.ds(96, 32))

    def first_copy(chunk):
        rows = chunks[chunk]
        if chunk % 2 == 0:
            source, peer = tri.at[:, 1 - x, rows], at_x
        else:
            source, peer = tri.at[1 - y, :, rows], at_y
        return remote(source, first_in.at[chunk], first_sem, (chunk,), peer)

    def second_copy(chunk):
        rows = chunks[chunk]
        if chunk % 2 == 0:
            source, peer = tri.at[1 - y, x, rows], at_y
        else:
            source, peer = tri.at[y, 1 - x, rows], at_x
        return remote(source, second_in.at[chunk], second_sem, (chunk,), peer)

    def line_rows(chunk):
        return pl.ds(pl.multiple_of(32 * (chunk // 2) + 64 * (chunk % 2), 32), 32)

    def to_left(chunk):
        rows = line_rows(chunk)
        return remote(to_left_buf.at[rows], right_in.at[rows], line_sem, (0, chunk), left)

    def to_right(chunk):
        rows = line_rows(chunk)
        return remote(to_right_buf.at[rows], left_in.at[rows], line_sem, (1, chunk), right)

    for chunk in range(4):
        first_copy(chunk).start()
    for chunk, rows in enumerate(chunks):
        first_copy(chunk).wait_recv()
        if chunk % 2 == 0:
            tri[1 - y, x, rows] = tri[1 - y, x, rows] + first_in[chunk, 1 - y]
        else:
            tri[y, 1 - x, rows] = tri[y, 1 - x, rows] + first_in[chunk, 1 - x]
        second_copy(chunk).start()

    @pl.when(z == 0)
    def _():
        left_in[...] = jnp.zeros_like(left_in)

    @pl.when(z == LINE - 1)
    def _():
        right_in[...] = jnp.zeros_like(right_in)

    for turn in range(LINE + 3):
        if turn < 4:
            rows = chunks[turn]
            second_copy(turn).wait_recv()
            near = first_in[turn, y] if turn % 2 == 0 else first_in[turn, x]
            total[rows] = (tri[y, x, rows] + near) + second_in[turn]
        chunk = turn - z

        @pl.when(jnp.logical_and(chunk >= 0, chunk < 4))
        def _():
            @pl.when(z > 0)
            def _():
                to_right(chunk).wait_recv()

            @pl.when(z < LINE - 1)
            def _():
                rows = line_rows(chunk)
                to_right_buf[rows] = total[rows] + left_in[rows]
                to_right(chunk).start()

        other = turn - (LINE - 1 - z)

        @pl.when(jnp.logical_and(other >= 0, other < 4))
        def _():
            @pl.when(z < LINE - 1)
            def _():
                to_left(other).wait_recv()

            @pl.when(z > 0)
            def _():
                rows = line_rows(other)
                to_left_buf[rows] = total[rows] + right_in[rows]
                to_left(other).start()

    tri_unpack(total[...] + left_in[...] + right_in[...], square)
    tri_pack(factor_ref, (y, x), newton_schulz(square))

    def spread(row, column, part, way, peer):
        block = factor_ref.at[row, column, part]
        index = 2 * way + (0 if part is part_a else 1)
        return remote(block, block, spread_sem, (index,), peer)

    own_y = [spread(y, x, part, 0, at_y) for part in (part_a, part_b)]
    own_x = [spread(y, x, part, 1, at_x) for part in (part_a, part_b)]
    own_y[0].start()
    own_x[1].start()
    own_y[1].start()
    own_x[0].start()
    spread(1 - y, x, part_a, 0, at_y).wait_recv()
    onward_a = spread(1 - y, x, part_a, 2, at_x)
    onward_a.start()
    spread(y, 1 - x, part_b, 1, at_x).wait_recv()
    onward_b = spread(y, 1 - x, part_b, 2, at_y)
    onward_b.start()
    spread(1 - y, x, part_b, 0, at_y).wait_recv()
    spread(y, 1 - x, part_a, 1, at_x).wait_recv()
    spread(1 - y, 1 - x, part_a, 2, at_x).wait_recv()
    spread(1 - y, 1 - x, part_b, 2, at_y).wait_recv()

    for copy in (*own_y, *own_x, onward_a, onward_b):
        copy.wait_send()
    for chunk in range(4):
        first_copy(chunk).wait_send()
        second_copy(chunk).wait_send()

        @pl.when(z > 0)
        def _():
            to_left(chunk).wait_send()

        @pl.when(z < LINE - 1)
        def _():
            to_right(chunk).wait_send()


def muon_factors(own, stat, moments):
    in_vmem = pl.BlockSpec(memory_space=pltpu.VMEM)
    width = own.shape[1]
    return pl.pallas_call(
        muon_kernel,
        out_shape=jax.ShapeDtypeStruct((2, 2, 128, 768), FL),
        in_specs=[in_vmem] * 6,
        out_specs=in_vmem,
        scratch_shapes=[
            pltpu.VMEM((128, width), FL),
            pltpu.VMEM((2, 2, 128, 768), FL),
            pltpu.VMEM((4, 2, 32, 768), FL),
            pltpu.VMEM((4, 32, 768), FL),
            pltpu.VMEM((128, 768), FL),
            pltpu.VMEM((128, 768), FL),
            pltpu.VMEM((128, 768), FL),
            pltpu.VMEM((128, 768), FL),
            pltpu.VMEM((128, 768), FL),
            pltpu.VMEM((width, width), FL),
            pltpu.SemaphoreType.DMA((2, 4)),
            pltpu.SemaphoreType.DMA((2, 4)),
            pltpu.SemaphoreType.DMA((2, 2, 4)),
            pltpu.SemaphoreType.DMA((2, 6)),
        ],
        compiler_params=pltpu.CompilerParams(
            collective_id=2, has_side_effects=True, vmem_limit_bytes=40 * 2**20
        ),
        name="muon_factors",
    )(own, stat, *moments)


def update_kernel(scales, *refs):
    own_ref, other_ref, stat_ref, factor_ref = refs[:4]
    mats, moments, smalls, firsts, seconds = [refs[4 + 4 * at : 8 + 4 * at] for at in range(5)]
    scalar_out = refs[24]
    new_mats, new_moms, new_ws, new_fs, new_ss = [
        refs[25 + 4 * at : 29 + 4 * at] for at in range(5)
    ]
    padded, square = refs[45:47]
    first_core = lax.axis_index("mp") == 0
    stat = stat_ref[...]
    weight_total, grad_norm, scaling = clip_scale(stat)
    row = lax.broadcasted_iota(jnp.int32, (8, 128), 0)
    loss_total = jnp.sum(stat[0:1], keepdims=True)
    scalar_out[...] = jnp.where(row == 0, loss_total, jnp.where(row == 1, weight_total, grad_norm))
    counts = [ref.shape[0] for ref in mats]
    for index in range(4):
        rate = MUON_RATES[index]
        new_moms[index][...] = new_moment(
            index, counts, own_ref, scaling, moments[index], padded
        )
        tri_unpack(factor_ref[index // 2, index % 2], square)
        change = product(padded[...], square[...])[: counts[index]]
        new_mats[index][...] = (
            mats[index][...] * (1.0 - rate * DECAY) - rate * scales[index] * change
        )

    lead = sum(counts)
    patch_rows, head_rows = smalls[0].shape[0], smalls[1].shape[0]
    tokens = smalls[2].shape[1]
    classes = smalls[1].shape[1]

    def adam(index, grad, rows, lanes):
        spot = (rows, lanes)
        rate = ADAM_RATES[index]
        grad = grad * scaling
        first = BETA_ONE * firsts[index][spot] + (1.0 - BETA_ONE) * grad
        second = BETA_TWO * seconds[index][spot] + (1.0 - BETA_TWO) * grad * grad
        step_size = (
            first / (1.0 - BETA_ONE**STEP) / (jnp.sqrt(second / (1.0 - BETA_TWO**STEP)) + ADAM_EPS)
        )
        new_ws[index][spot] = smalls[index][spot] * (1.0 - rate * DECAY) - rate * step_size
        new_fs[index][spot] = first
        new_ss[index][spot] = second

    def taken(at, count, from_first):
        mine, other = own_ref[lead + at : lead + at + count], other_ref[at : at + count]
        return jnp.where(first_core, mine, other) if from_first else jnp.where(
            first_core, other, mine
        )

    every = slice(None)
    adam(0, taken(0, patch_rows, True), every, every)
    tables = taken(patch_rows, head_rows, True)
    adam(2, tables[:, :tokens], every, every)
    at = tokens // 128 * 128
    gains = tables[:, at : at + 128].T
    at = tokens - at
    adam(3, gains[at : at + smalls[3].shape[0]], every, every)
    width = own_ref.shape[1]
    for part in range(-(-classes // width)):
        stop = min(classes, (part + 1) * width)
        grad = taken(part * head_rows, head_rows, False)[:, : stop - part * width]
        adam(1, grad, every, slice(part * width, stop))


def update_all(own, other, stat, factor, mats, moments, smalls, firsts, seconds):
    dp_size = lax.axis_size("dp")
    in_vmem = pl.BlockSpec(memory_space=pltpu.VMEM)
    width = own.shape[1]
    scales = [0.2 * math.sqrt(max(mat.shape[1], mat.shape[0] * dp_size)) for mat in mats]
    outs = [*mats, *mats, *smalls, *smalls, *smalls]
    got = pl.pallas_call(
        lambda *refs: update_kernel(scales, *refs),
        out_shape=[jax.ShapeDtypeStruct((8, 128), FL)]
        + [jax.ShapeDtypeStruct(part.shape, FL) for part in outs],
        in_specs=[in_vmem] * 24,
        out_specs=[in_vmem] * 21,
        scratch_shapes=[pltpu.VMEM((128, width), FL), pltpu.VMEM((width, width), FL)],
        compiler_params=pltpu.CompilerParams(vmem_limit_bytes=40 * 2**20),
        name="update_weights",
    )(own, other, stat, factor, *mats, *moments, *smalls, *firsts, *seconds)
    return (got[0][0, 0], got[0][1, 0], got[0][2, 0], got[1:])


def muon_factor(gram):
    size = jnp.sqrt(jnp.trace(gram)) + 1e-07
    square = gram / (size * size)
    unit = jnp.eye(gram.shape[0], dtype=FL)
    factor = None

    def times(left, right):
        return jnp.dot(left, right, precision=PRECISE)

    for turn in range(5):
        mixed = NS_A * unit + NS_B * square + NS_C * times(square, square)
        factor = mixed if factor is None else times(mixed, factor)
        if turn < 4:
            square = times(times(mixed, square), mixed)
    return factor / size


def update_plain(own, other, stat, mats, moments, smalls, firsts, seconds):
    dp_size = lax.axis_size("dp")
    mp_index = lax.axis_index("mp")
    loss_total = jnp.sum(stat[0])
    weight_total = jnp.sum(stat[1])
    grad_norm = jnp.sqrt(jnp.sum(stat[8:16])) / weight_total
    scaling = THRESHOLD / jnp.maximum(grad_norm, THRESHOLD) / weight_total
    new_moms = []
    at = 0
    for moment in moments:
        count = moment.shape[2]
        new_moms.append(MOMENTUM * moment + own[at : at + count].T[None] * scaling)
        at += count
    grams = lax.psum(
        jnp.stack([jnp.dot(mom[0], mom[0].T, precision=PRECISE) for mom in new_moms]), "dp"
    )
    new_mats = []
    for index, weight in enumerate(mats):
        rate = MUON_RATES[index]
        scale = 0.2 * math.sqrt(max(weight.shape[1], weight.shape[2] * dp_size))
        change = jnp.dot(muon_factor(grams[index]), new_moms[index][0], precision=PRECISE)
        new_mats.append(weight * (1.0 - rate * DECAY) - rate * scale * change[None])
    mine = own[at : at + other.shape[0]]
    core_first = jnp.where(mp_index == 0, mine, other)
    core_second = jnp.where(mp_index == 0, other, mine)
    patch_rows, head_rows = smalls[0].shape[0], smalls[1].shape[0]
    tokens = smalls[2].shape[1]
    tables = core_first[patch_rows : patch_rows + head_rows]
    head_grad = [
        core_second[at : at + head_rows]
        for at in range(0, core_second.shape[0] - head_rows + 1, head_rows)
    ]
    grads = (
        core_first[:patch_rows],
        jnp.concatenate(head_grad, 1)[:, : smalls[1].shape[1]],
        tables[:, :tokens],
        tables[:, tokens : tokens + smalls[3].shape[1]],
    )
    new_ws, new_fs, new_ss = ([], [], [])
    for index in range(4):
        grad = grads[index] * scaling
        rate = ADAM_RATES[index]
        first = BETA_ONE * firsts[index] + (1.0 - BETA_ONE) * grad
        second = BETA_TWO * seconds[index] + (1.0 - BETA_TWO) * grad * grad
        step_size = (
            first / (1.0 - BETA_ONE**STEP) / (jnp.sqrt(second / (1.0 - BETA_TWO**STEP)) + ADAM_EPS)
        )
        new_ws.append(smalls[index] * (1.0 - rate * DECAY) - rate * step_size)
        new_fs.append(first)
        new_ss.append(second)
    news = [*new_mats, *new_moms, *new_ws, *new_fs, *new_ss]
    return (loss_total, weight_total, grad_norm, news)


def body(
    pool_images,
    pick_rows,
    pick_weight,
    pick_label,
    in_proj,
    out_proj,
    up_proj,
    down_proj,
    in_moment,
    out_moment,
    up_moment,
    down_moment,
    patch_embed,
    class_head,
    pos_table,
    norm_params,
    patch_first,
    head_first,
    pos_first,
    norm_first,
    patch_second,
    head_second,
    pos_second,
    norm_second,
):
    mp_size = lax.axis_size("mp")
    mp_index = lax.axis_index("mp")
    dp_size = lax.axis_size("dp")
    mats = (in_proj, out_proj, up_proj, down_proj)
    smalls = (patch_embed, class_head, pos_table, norm_params)
    half = pool_images.shape[0] // mp_size
    images = lax.dynamic_slice_in_dim(pool_images, mp_index * half, half)
    fits = dp_size == GRID_DP and up_proj.shape[2] == SHARE
    if fits:
        tokens = pos_table.shape[1]
        padded = -(-tokens // 16) * 16
        images = jnp.pad(images, ((0, 0), (0, padded - images.shape[1]), (0, 0)))
        own, other, stat, score = whole_step(
            images,
            (pick_rows, pick_weight, pick_label),
            [mat[0].T for mat in mats],
            [*smalls[:3], norm_params.T],
        )
    else:
        own_rows = mp_index * half + jnp.arange(half, dtype=jnp.int32)
        chosen = (pick_rows[None] == own_rows[:, None]).astype(FL) * pick_weight.astype(FL)[None]
        counts = jnp.sum(chosen, 1)
        classes = jnp.arange(class_head.shape[1], dtype=jnp.int32)
        is_target = (pick_label[:, None] == classes[None]).astype(FL)
        target_weight = jnp.sum(chosen[:, :, None] * is_target[None], 1)

        whole, table = gather_weights(mats, *smalls)
        small_rows = whole.shape[2] - sum([mat.shape[2] for mat in mats]) - 8
        fetched = unpack_weights(whole, table, mats, *smalls)
        loss, score, d_mats, d_patch, d_head, d_pos, d_norm = local_step(
            images, counts, target_weight, fetched
        )
        parts = pack_gradients(d_mats, d_patch, d_head, d_pos, d_norm, small_rows)
        stat = jnp.zeros((8, 128), FL).at[0, 0].set(loss).at[1, 0].set(jnp.sum(counts))
        own, other, stat = reduce_gradients(parts, small_rows, stat)
    moments = (in_moment, out_moment, up_moment, down_moment)
    firsts = (patch_first, head_first, pos_first, norm_first)
    seconds = (patch_second, head_second, pos_second, norm_second)
    if fits:
        turned = [[part[0].T for part in group] for group in (mats, moments)]
        factor = muon_factors(own, stat, turned[1])
        groups = [[*group[:3], group[3].T] for group in (smalls, firsts, seconds)]
        loss_total, weight_total, grad_norm, news = update_all(
            own, other, stat, factor, *turned, *groups
        )
        news = [part.T[None] for part in news[:8]] + [
            part.T if index % 4 == 3 else part for index, part in enumerate(news[8:])
        ]
    else:
        loss_total, weight_total, grad_norm, news = update_plain(
            own, other, stat, mats, moments, smalls, firsts, seconds
        )
    return (loss_total, weight_total, grad_norm, score, *news)


def solution(mesh):
    mat = P("mp", None, "dp")
    row = P("dp", None)
    in_specs = (P("dp", None, None), P("dp"), P("dp"), P("dp")) + (mat,) * 8 + (row,) * 12
    out_specs = (P(), P(), P(), P(("dp", "mp"))) + (mat,) * 8 + (row,) * 12
    return jax.shard_map(body, mesh=mesh, in_specs=in_specs, out_specs=out_specs, check_vma=False)
```

profile of v0, /device:TPU:0, one launch (start us, length us, event | category | flops | bytes accessed | tf_op | source)
XLA Modules:
  0.0 237.2 jit_solution(16064125031520685703)
XLA Ops:
  0.7 2.3 constant_dynamic-slice_fusion
  3.0 0.1 copy.50
  3.1 1.1 pad.4.refs_0_
  4.3 0.0 copy-start.2
  4.3 169.4 %forward_backward.1 = (f32[384,384]{1,0:T(8,128)}, f32[96,384]{1,0:T(8,128)}, f32[16,128]{1,0:T(8,128)}, f32[16,128]{1,0:T(8,128)}) custom-call(bf16[4,208,768]{2,1,0:T(8,128)(2,1)} %pad.4.refs_0_, s32[8]{0:T(128)} %refs_1_.1, s32[8]{0:T(128)} %refs_2_.1, s32[8]{0:T(128)} %refs_3_.1, f32[72,384]{1,0:T(8,128)} %bitcast.65, f32[24,384]{1,0:T(8,128)} %bitcast.69, ...), custom_call_target="tpu_custom_call" | custom-call | tf_op jit(solution)/shard_map/forward_backward/pallas_call | solution.py:1153
  173.7 1.3 slice_reduce_fusion
  175.0 0.0 copy-done.2
  175.0 0.0 copy-done.3
  175.0 0.0 copy-done.7
  175.0 0.0 copy-done.12
  175.0 0.0 copy-start
  175.0 1.1 copy-done
  176.1 0.7 copy-done.19
  176.8 0.0 copy-start.8
  176.8 0.0 copy-start.9
  176.8 0.0 copy-start.10
  176.8 0.0 copy-start.11
  176.8 0.0 copy-start.13
  176.8 0.0 copy-start.14
  176.8 0.0 copy-start.15
  176.8 0.0 copy-start.16
  176.9 0.0 copy-start.17
  176.9 0.0 copy-start.18
  176.9 0.0 copy-start.20
  176.9 0.0 copy-start.21
  176.9 0.0 copy-start.22
  176.9 0.0 copy-start.23
  176.9 57.4 %muon_factors.1.refs_3_ = f32[2,2,128,768]{3,2,1,0:T(8,128)S(1)} custom-call(f32[384,384]{1,0:T(8,128)S(1)} %copy-done, f32[16,128]{1,0:T(8,128)S(1)} %copy-done.19, f32[72,384]{1,0:T(8,128)S(1)} %bitcast.67, f32[24,384]{1,0:T(8,128)S(1)} %bitcast.71, f32[96,384]{1,0:T(8,128)S(1)} %bitcast.57, f32[96,384]{1,0:T(8,128)S(1)} %bitcast.59), custom_call_target="tpu_custom_call" | custom-call | tf_op jit(solution)/shard_map/muon_factors/pallas_call | solution.py:1493
  234.3 0.0 copy-done.1
  234.3 0.0 copy-done.4
  234.3 0.0 copy-done.5
  234.3 0.0 copy-done.6
  234.3 0.0 copy-done.8
  234.3 0.0 copy-done.9
  234.3 0.0 copy-done.10
  234.4 0.0 copy-done.11
  234.4 0.0 copy-done.13
  234.4 0.0 copy-done.14
  234.4 0.0 copy-done.15
  234.4 0.0 copy-done.16
  234.4 0.0 copy-done.17
  234.4 0.0 copy-done.18
  234.4 0.0 copy-done.20
  234.4 0.0 copy-done.21
  234.4 0.0 copy-done.22
  234.5 0.0 copy-done.23
  234.5 2.0 update_weights.1
  236.4 0.5 fusion
  (8 shorter events, 0.0 us)
Async XLA Ops:
  4.3 170.7 %copy-start.2 = (f32[1,384,96]{1,2,0:T(8,128)S(1)}, f32[1,384,96]{1,2,0:T(8,128)}, u32[]{:S(2)}) copy-start(f32[1,384,96]{1,2,0:T(8,128)} %param.34) | copy-start | bytes 442372
  4.3 170.7 %copy-start.3 = (f32[1,384,96]{1,2,0:T(8,128)S(1)}, f32[1,384,96]{1,2,0:T(8,128)}, u32[]{:S(2)}) copy-start(f32[1,384,96]{1,2,0:T(8,128)} %param.35) | copy-start | bytes 442372
  4.3 170.7 %copy-start.7 = (f32[1,384,72]{1,2,0:T(8,128)S(1)}, f32[1,384,72]{1,2,0:T(8,128)}, u32[]{:S(2)}) copy-start(f32[1,384,72]{1,2,0:T(8,128)} %param.32) | copy-start | bytes 331780
  4.3 170.7 %copy-start.12 = (f32[1,384,24]{1,2,0:T(8,128)S(1)}, f32[1,384,24]{1,2,0:T(8,128)}, u32[]{:S(2)}) copy-start(f32[1,384,24]{1,2,0:T(8,128)} %param.33) | copy-start | bytes 110596
  175.0 1.1 copy-start
  176.1 0.7 copy-start.19
  176.7 57.5 %copy-start.1 = (f32[384,384]{1,0:T(8,128)S(1)}, f32[384,384]{1,0:T(8,128)}, u32[]{:S(2)}) copy-start(f32[384,384]{1,0:T(8,128)} %get-tuple-element.49.own_ref.refs_0_) | copy-start | bytes 1769476
  176.8 57.5 %copy-start.4 = (f32[1,384,96]{1,2,0:T(8,128)S(1)}, f32[1,384,96]{1,2,0:T(8,128)}, u32[]{:S(2)}) copy-start(f32[1,384,96]{1,2,0:T(8,128)} %param.30) | copy-start | bytes 442372
  176.8 57.6 %copy-start.5 = (f32[1,384,96]{1,2,0:T(8,128)S(1)}, f32[1,384,96]{1,2,0:T(8,128)}, u32[]{:S(2)}) copy-start(f32[1,384,96]{1,2,0:T(8,128)} %param.31) | copy-start | bytes 442372
  176.8 57.6 %copy-start.6 = (f32[1,384,72]{1,2,0:T(8,128)S(1)}, f32[1,384,72]{1,2,0:T(8,128)}, u32[]{:S(2)}) copy-start(f32[1,384,72]{1,2,0:T(8,128)} %param.28) | copy-start | bytes 331780
  176.8 57.6 %copy-start.8 = (f32[24,1000]{1,0:T(8,128)S(1)}, f32[24,1000]{1,0:T(8,128)}, u32[]{:S(2)}) copy-start(f32[24,1000]{1,0:T(8,128)} %refs_13_.1) | copy-start | bytes 288004
  176.8 57.6 %copy-start.9 = (f32[48,384]{1,0:T(8,128)S(1)}, f32[48,384]{1,0:T(8,128)}, u32[]{:S(2)}) copy-start(f32[48,384]{1,0:T(8,128)} %refs_12_.1) | copy-start | bytes 221188
  176.8 57.6 %copy-start.10 = (f32[96,384]{1,0:T(8,128)S(1)}, f32[96,384]{1,0:T(8,128)}, u32[]{:S(2)}) copy-start(f32[96,384]{1,0:T(8,128)} %get-tuple-element.50.refs_1_) | copy-start | bytes 442372
  176.8 57.6 %copy-start.11 = (f32[1,384,24]{1,2,0:T(8,128)S(1)}, f32[1,384,24]{1,2,0:T(8,128)}, u32[]{:S(2)}) copy-start(f32[1,384,24]{1,2,0:T(8,128)} %param.29) | copy-start | bytes 110596
  176.8 57.6 %copy-start.13 = (f32[24,197]{1,0:T(8,128)S(1)}, f32[24,197]{1,0:T(8,128)}, u32[]{:S(2)}) copy-start(f32[24,197]{1,0:T(8,128)} %refs_14_.1) | copy-start | bytes 56740
  176.8 57.6 %copy-start.14 = (f32[24,1000]{1,0:T(8,128)S(1)}, f32[24,1000]{1,0:T(8,128)}, u32[]{:S(2)}) copy-start(f32[24,1000]{1,0:T(8,128)} %refs_17_.1) | copy-start | bytes 288004
  176.8 57.6 %copy-start.15 = (f32[24,1000]{1,0:T(8,128)S(1)}, f32[24,1000]{1,0:T(8,128)}, u32[]{:S(2)}) copy-start(f32[24,1000]{1,0:T(8,128)} %refs_21_.1) | copy-start | bytes 288004
  176.8 57.6 %copy-start.16 = (f32[48,384]{1,0:T(8,128)S(1)}, f32[48,384]{1,0:T(8,128)}, u32[]{:S(2)}) copy-start(f32[48,384]{1,0:T(8,128)} %refs_16_.1) | copy-start | bytes 221188
  176.9 57.6 %copy-start.17 = (f32[48,384]{1,0:T(8,128)S(1)}, f32[48,384]{1,0:T(8,128)}, u32[]{:S(2)}) copy-start(f32[48,384]{1,0:T(8,128)} %refs_20_.1) | copy-start | bytes 221188
  176.9 57.6 %copy-start.18 = (f32[24,10]{0,1:T(8,128)S(1)}, f32[24,10]{0,1:T(8,128)}, u32[]{:S(2)}) copy-start(f32[24,10]{0,1:T(8,128)} %param.39) | copy-start | bytes 2884
  176.9 57.5 %copy-start.20 = (f32[24,197]{1,0:T(8,128)S(1)}, f32[24,197]{1,0:T(8,128)}, u32[]{:S(2)}) copy-start(f32[24,197]{1,0:T(8,128)} %refs_18_.1) | copy-start | bytes 56740
  176.9 57.5 %copy-start.21 = (f32[24,197]{1,0:T(8,128)S(1)}, f32[24,197]{1,0:T(8,128)}, u32[]{:S(2)}) copy-start(f32[24,197]{1,0:T(8,128)} %refs_22_.1) | copy-start | bytes 56740
  176.9 57.5 %copy-start.22 = (f32[24,10]{0,1:T(8,128)S(1)}, f32[24,10]{0,1:T(8,128)}, u32[]{:S(2)}) copy-start(f32[24,10]{0,1:T(8,128)} %param.43) | copy-start | bytes 2884
  176.9 57.5 %copy-start.23 = (f32[24,10]{0,1:T(8,128)S(1)}, f32[24,10]{0,1:T(8,128)}, u32[]{:S(2)}) copy-start(f32[24,10]{0,1:T(8,128)} %param.47) | copy-start | bytes 2884
where the time goes:
time: 240 us; the launch traced here: 237 us
  Pallas kernels  229 us (95%)
  local copies, waits for them, and re-layouts  7.28 us (3%)
    pallas_call x1, Pallas kernels, whole_step(): pl.pallas_call(lambda *refs: step_kernel(tokens, classes, *refs), out_sha...  169 us
    pallas_call x1, Pallas kernels, muon_factors(): pl.pallas_call(muon_kernel, out_shape=jax.ShapeDtypeStruct((2, 2, 128, 76...  57.4 us

commit v1 on v0

--- a/solution.py
+++ b/solution.py
@@ -63,8 +63,8 @@
 LINE = 4
 GRID_DP = 16
 SHARE = 96
-FETCH_SLOTS = (0, 8, 16, 24)
-JOB_SLOTS = (0, 10, 18)
+FETCH_PLAN = ((0, 2), (2, 2), (6, 3), (12, 4))
+JOB_PLAN = ((0, 4), (10, 4), (18, 4), (30, 2))
 
 
 def place():
@@ -456,18 +456,11 @@
 
     def serve(slot, jobs):
         for job in jobs:
-            age = slot - JOB_SLOTS[job]
-            due(age, stage_core, job)
-            due(age - 2, stage_first, job)
-            due(age - 5 - middle, stage_second, job)
-
-    def serve_static(job, turn):
-        if turn < LINE:
-            stage_core(job, dest(turn))
-        if 1 <= turn < LINE + 1:
-            stage_first(job, dest(turn - 1))
-        if turn >= 2:
-            stage_second(job, dest(turn - 2))
+            start, stride = JOB_PLAN[job]
+            age = slot - start
+            due(age, stride, stage_core, job)
+            due(age - stride, stride, stage_first, job)
+            due(age - 2 * stride - 1 - middle, stride, stage_second, job)
 
     def swap(job):
         rows = rows_of(job, c)
@@ -592,22 +585,24 @@
         block_landed(job, d, item(1 - near, 1 - far), fetch_near_sem.at[1, job, d, 1])
         fetch_core(job, d).start()
 
-    def due(age, stage, job, nearest_first=False):
+    def due(age, stride, stage, job, nearest_first=False):
         def act(turn):
             stage(job, dest(LINE - 1 - turn if nearest_first else turn))
 
         if isinstance(age, int):
-            if age % 2 == 0 and 0 <= age < 2 * LINE:
-                act(age // 2)
+            if age % stride == 0 and 0 <= age < stride * LINE:
+                act(age // stride)
             return
-
-        @pl.when(jnp.logical_and(age % 2 == 0, jnp.logical_and(age >= 0, age < 2 * LINE)))
-        def _():
-            act(age // 2)
+        now = jnp.logical_and(age >= 0, age < stride * LINE)
+
+        @pl.when(jnp.logical_and(now, age % stride == 0))
+        def _():
+            act(age // stride)
 
     def fetch(slot, jobs):
         for job in jobs:
-            age = slot - FETCH_SLOTS[job]
+            start, stride = FETCH_PLAN[job]
+            age = slot - start
             if isinstance(age, int):
                 if age == 0:
                     fetch_begin(job)
@@ -617,9 +612,9 @@
                 def _():
                     fetch_begin(job)
 
-            due(age - edge, stage_line, job, True)
-            due(age - 2 - edge, stage_far, job, True)
-            due(age - 4 - edge, stage_near, job, True)
+            due(age - edge, stride, stage_line, job, True)
+            due(age - stride - edge, stride, stage_far, job, True)
+            due(age - 2 * stride - edge, stride, stage_near, job, True)
 
     def fetch_ready(job):
         for d in range(LINE):
@@ -681,7 +676,7 @@
         pack[share : 2 * share] = up_ref[...].astype(BF)
 
     for slot in range(12):
-        fetch(slot, (0, 1))
+        fetch(slot, (0, 1, 2))
         if slot == 0:
 
             @pl.when(c == 0)
@@ -785,9 +780,9 @@
                 mixed = one_head(jnp.dot(prob, value, preferred_element_type=FL))
                 attended[layer, i, :, at : at + 128] = mixed.astype(BF)
                 if pair == 1:
-                    fetch(12 + 16 * layer + 2 * i, (1, 2) if layer == 0 else (3,))
+                    fetch(12 + 16 * layer + 2 * i, (1, 2, 3) if layer == 0 else (3,))
             resid[i] = values + along(attended[layer, i], w_out[layer], 1, 1)
-            fetch(13 + 16 * layer + 2 * i, (1, 2) if layer == 0 else (3,))
+            fetch(13 + 16 * layer + 2 * i, (1, 2, 3) if layer == 0 else (3,))
             return carry
 
         lax.fori_loop(0, image_count, forward, 0)
@@ -930,8 +925,6 @@
             return carry
 
         lax.fori_loop(0, image_count, back_mlp, 0)
-        if layer < layers - 1:
-            job_finish(0)
         few = per // 2
         for part in range(2 * parts):
             lanes = slice(part * width, (part + 1) * width)
@@ -949,12 +942,12 @@
                 few, n_up, width
             )
             if layer < layers - 1:
-                serve(14 + part, (1,))
+                serve(14 + part, (0, 1))
 
         job = 2 * (layers - 1 - layer)
         job_start(job)
         first_slot = 18 * (layers - 1 - layer)
-        jobs = (0,) if layer == layers - 1 else (1, 2)
+        jobs = (0,) if layer == layers - 1 else (0, 1, 2)
 
         def back_attention(i, carry):
             grad = resid[i]
@@ -992,15 +985,13 @@
             return carry
 
         lax.fori_loop(0, image_count, back_attention, 0)
-        if layer < layers - 1:
-            job_finish(1)
         for part in range(3):
             lanes = slice(part * width, (part + 1) * width)
             flat[lanes] = along(
                 all_rows(active, layer, every, every, lanes), all_rows(rows_a, layer), 0, 0
             )
             if part > 0:
-                serve(first_slot + 7 + part, jobs[-1:])
+                serve(first_slot + 7 + part, jobs)
         flat[3 * width :] = along(all_rows(upper, every), all_rows(attended, layer), 0, 0)
 
         def pack_mats(k, carry):
@@ -1017,6 +1008,8 @@
         lax.fori_loop(0, dp_size, pack_mats, 0)
         if layer > 0:
             job_start(1)
+        else:
+            job_finish(0)
 
     places[...] = jnp.zeros_like(places)
 
@@ -1036,7 +1029,7 @@
         work[0, part * per_patch : (part + 1) * per_patch, lead : lead + patch_rows] = grad.astype(
             BF
         ).reshape(per_patch, patch_rows, width)
-        serve(28 + part, (2,))
+        serve(28 + part, (1, 2))
     table[...] = jnp.zeros_like(table)
     table[0:1] = places[tokens - 1 : tokens]
     table[1:tokens] = places[0 : tokens - 1]
@@ -1051,11 +1044,11 @@
         return carry
 
     lax.fori_loop(0, dp_size, pack_table, 0)
-    serve(30, (2,))
     job_start(3)
+    for slot in range(30, 43):
+        serve(slot, (1, 2, 3))
+    job_finish(1)
     job_finish(2)
-    for turn in range(LINE + 2):
-        serve_static(3, turn)
     job_finish(3)
 
     def small_copy():

time: 240 us -> 223 us (0.929)
  Pallas kernels: 229 us -> 212 us
    pallas_call x1, Pallas kernels: 169 us -> 153 us  [whole_step(): pl.pallas_call(lambda *refs: step_kernel(tokens, classes, *refs), out_sha...]
where the time goes in v1:
time: 223 us; the launch traced here: 220 us
  Pallas kernels  212 us (95%)
  local copies, waits for them, and re-layouts  7.28 us (3%)
    pallas_call x1, Pallas kernels, whole_step(): pl.pallas_call(lambda *refs: step_kernel(tokens, classes, *refs), out_sha...  153 us
    pallas_call x1, Pallas kernels, muon_factors(): pl.pallas_call(muon_kernel, out_shape=jax.ShapeDtypeStruct((2, 2, 128, 76...  57.1 us

profile of v1, /device:TPU:0, one launch (start us, length us, event | category | flops | bytes accessed | tf_op | source)
XLA Modules:
  0.0 220.2 jit_solution(5371553509681838163)
XLA Ops:
  0.7 2.3 %constant_dynamic-slice_fusion = bf16[4,196,768]{2,0,1:T(4,128)(2,1)S(1)} fusion(bf16[8,196,768]{2,0,1:T(8,128)(2,1)} %param.24, s32[]{:T(128)S(6)} %select_n.3), kind=kLoop, calls=%fused_computation.1 | loop fusion | bytes 2408452 | tf_op jit(solution)/shard_map/dynamic_slice | solution.py:1701
  3.0 0.1 copy.50
  3.1 1.1 pad.4.refs_0_
  4.3 0.0 copy-start.2
  4.3 152.6 %forward_backward.1 = (f32[384,384]{1,0:T(8,128)}, f32[96,384]{1,0:T(8,128)}, f32[16,128]{1,0:T(8,128)}, f32[16,128]{1,0:T(8,128)}) custom-call(bf16[4,208,768]{2,1,0:T(8,128)(2,1)} %pad.4.refs_0_, s32[8]{0:T(128)} %refs_1_.1, s32[8]{0:T(128)} %refs_2_.1, s32[8]{0:T(128)} %refs_3_.1, f32[72,384]{1,0:T(8,128)} %bitcast.65, f32[24,384]{1,0:T(8,128)} %bitcast.69, ...), custom_call_target="tpu_custom_call" | custom-call | tf_op jit(solution)/shard_map/forward_backward/pallas_call | solution.py:1146
  156.8 1.3 slice_reduce_fusion
  158.1 0.0 copy-done.2
  158.2 0.0 copy-done.3
  158.2 0.0 copy-done.7
  158.2 0.0 copy-done.12
  158.2 0.0 copy-start
  158.2 1.1 copy-done
  159.2 0.7 copy-done.19
  159.9 0.0 copy-start.8
  159.9 0.0 copy-start.9
  160.0 0.0 copy-start.10
  160.0 0.0 copy-start.11
  160.0 0.0 copy-start.13
  160.0 0.0 copy-start.14
  160.0 0.0 copy-start.15
  160.0 0.0 copy-start.16
  160.0 0.0 copy-start.17
  160.0 0.0 copy-start.18
  160.1 0.0 copy-start.20
  160.1 0.0 copy-start.21
  160.1 0.0 copy-start.22
  160.1 0.0 copy-start.23
  160.1 57.1 %muon_factors.1.refs_3_ = f32[2,2,128,768]{3,2,1,0:T(8,128)S(1)} custom-call(f32[384,384]{1,0:T(8,128)S(1)} %copy-done, f32[16,128]{1,0:T(8,128)S(1)} %copy-done.19, f32[72,384]{1,0:T(8,128)S(1)} %bitcast.67, f32[24,384]{1,0:T(8,128)S(1)} %bitcast.71, f32[96,384]{1,0:T(8,128)S(1)} %bitcast.57, f32[96,384]{1,0:T(8,128)S(1)} %bitcast.59), custom_call_target="tpu_custom_call" | custom-call | tf_op jit(solution)/shard_map/muon_factors/pallas_call | solution.py:1486
  217.2 0.0 copy-done.1
  217.3 0.0 copy-done.4
  217.3 0.0 copy-done.5
  217.3 0.0 copy-done.6
  217.3 0.0 copy-done.8
  217.3 0.0 copy-done.9
  217.3 0.0 copy-done.10
  217.3 0.0 copy-done.11
  217.3 0.0 copy-done.13
  217.3 0.0 copy-done.14
  217.3 0.0 copy-done.15
  217.4 0.0 copy-done.16
  217.4 0.0 copy-done.17
  217.4 0.0 copy-done.18
  217.4 0.0 copy-done.20
  217.4 0.0 copy-done.21
  217.4 0.0 copy-done.22
  217.4 0.0 copy-done.23
  217.4 2.0 update_weights.1
  219.4 0.5 fusion
  (8 shorter events, 0.0 us)
Async XLA Ops:
  4.3 153.9 %copy-start.2 = (f32[1,384,96]{1,2,0:T(8,128)S(1)}, f32[1,384,96]{1,2,0:T(8,128)}, u32[]{:S(2)}) copy-start(f32[1,384,96]{1,2,0:T(8,128)} %param.34) | copy-start | bytes 442372
  4.3 153.9 %copy-start.3 = (f32[1,384,96]{1,2,0:T(8,128)S(1)}, f32[1,384,96]{1,2,0:T(8,128)}, u32[]{:S(2)}) copy-start(f32[1,384,96]{1,2,0:T(8,128)} %param.35) | copy-start | bytes 442372
  4.3 153.9 %copy-start.7 = (f32[1,384,72]{1,2,0:T(8,128)S(1)}, f32[1,384,72]{1,2,0:T(8,128)}, u32[]{:S(2)}) copy-start(f32[1,384,72]{1,2,0:T(8,128)} %param.32) | copy-start | bytes 331780
  4.3 153.9 %copy-start.12 = (f32[1,384,24]{1,2,0:T(8,128)S(1)}, f32[1,384,24]{1,2,0:T(8,128)}, u32[]{:S(2)}) copy-start(f32[1,384,24]{1,2,0:T(8,128)} %param.33) | copy-start | bytes 110596
  158.2 1.1 copy-start
  159.2 0.7 copy-start.19
  159.9 57.3 %copy-start.1 = (f32[384,384]{1,0:T(8,128)S(1)}, f32[384,384]{1,0:T(8,128)}, u32[]{:S(2)}) copy-start(f32[384,384]{1,0:T(8,128)} %get-tuple-element.49.own_ref.refs_0_) | copy-start | bytes 1769476
  159.9 57.3 %copy-start.4 = (f32[1,384,96]{1,2,0:T(8,128)S(1)}, f32[1,384,96]{1,2,0:T(8,128)}, u32[]{:S(2)}) copy-start(f32[1,384,96]{1,2,0:T(8,128)} %param.30) | copy-start | bytes 442372
  159.9 57.3 %copy-start.5 = (f32[1,384,96]{1,2,0:T(8,128)S(1)}, f32[1,384,96]{1,2,0:T(8,128)}, u32[]{:S(2)}) copy-start(f32[1,384,96]{1,2,0:T(8,128)} %param.31) | copy-start | bytes 442372
  159.9 57.3 %copy-start.6 = (f32[1,384,72]{1,2,0:T(8,128)S(1)}, f32[1,384,72]{1,2,0:T(8,128)}, u32[]{:S(2)}) copy-start(f32[1,384,72]{1,2,0:T(8,128)} %param.28) | copy-start | bytes 331780
  159.9 57.4 %copy-start.8 = (f32[24,1000]{1,0:T(8,128)S(1)}, f32[24,1000]{1,0:T(8,128)}, u32[]{:S(2)}) copy-start(f32[24,1000]{1,0:T(8,128)} %refs_13_.1) | copy-start | bytes 288004
  159.9 57.4 %copy-start.9 = (f32[48,384]{1,0:T(8,128)S(1)}, f32[48,384]{1,0:T(8,128)}, u32[]{:S(2)}) copy-start(f32[48,384]{1,0:T(8,128)} %refs_12_.1) | copy-start | bytes 221188
  160.0 57.3 %copy-start.10 = (f32[96,384]{1,0:T(8,128)S(1)}, f32[96,384]{1,0:T(8,128)}, u32[]{:S(2)}) copy-start(f32[96,384]{1,0:T(8,128)} %get-tuple-element.50.refs_1_) | copy-start | bytes 442372
  160.0 57.3 %copy-start.11 = (f32[1,384,24]{1,2,0:T(8,128)S(1)}, f32[1,384,24]{1,2,0:T(8,128)}, u32[]{:S(2)}) copy-start(f32[1,384,24]{1,2,0:T(8,128)} %param.29) | copy-start | bytes 110596
  160.0 57.3 %copy-start.13 = (f32[24,197]{1,0:T(8,128)S(1)}, f32[24,197]{1,0:T(8,128)}, u32[]{:S(2)}) copy-start(f32[24,197]{1,0:T(8,128)} %refs_14_.1) | copy-start | bytes 56740
  160.0 57.3 %copy-start.14 = (f32[24,1000]{1,0:T(8,128)S(1)}, f32[24,1000]{1,0:T(8,128)}, u32[]{:S(2)}) copy-start(f32[24,1000]{1,0:T(8,128)} %refs_17_.1) | copy-start | bytes 288004
  160.0 57.3 %copy-start.15 = (f32[24,1000]{1,0:T(8,128)S(1)}, f32[24,1000]{1,0:T(8,128)}, u32[]{:S(2)}) copy-start(f32[24,1000]{1,0:T(8,128)} %refs_21_.1) | copy-start | bytes 288004
  160.0 57.3 %copy-start.16 = (f32[48,384]{1,0:T(8,128)S(1)}, f32[48,384]{1,0:T(8,128)}, u32[]{:S(2)}) copy-start(f32[48,384]{1,0:T(8,128)} %refs_16_.1) | copy-start | bytes 221188
  160.0 57.3 %copy-start.17 = (f32[48,384]{1,0:T(8,128)S(1)}, f32[48,384]{1,0:T(8,128)}, u32[]{:S(2)}) copy-start(f32[48,384]{1,0:T(8,128)} %refs_20_.1) | copy-start | bytes 221188
  160.0 57.3 %copy-start.18 = (f32[24,10]{0,1:T(8,128)S(1)}, f32[24,10]{0,1:T(8,128)}, u32[]{:S(2)}) copy-start(f32[24,10]{0,1:T(8,128)} %param.39) | copy-start | bytes 2884
  160.1 57.3 %copy-start.20 = (f32[24,197]{1,0:T(8,128)S(1)}, f32[24,197]{1,0:T(8,128)}, u32[]{:S(2)}) copy-start(f32[24,197]{1,0:T(8,128)} %refs_18_.1) | copy-start | bytes 56740
  160.1 57.3 %copy-start.21 = (f32[24,197]{1,0:T(8,128)S(1)}, f32[24,197]{1,0:T(8,128)}, u32[]{:S(2)}) copy-start(f32[24,197]{1,0:T(8,128)} %refs_22_.1) | copy-start | bytes 56740
  160.1 57.3 %copy-start.22 = (f32[24,10]{0,1:T(8,128)S(1)}, f32[24,10]{0,1:T(8,128)}, u32[]{:S(2)}) copy-start(f32[24,10]{0,1:T(8,128)} %param.43) | copy-start | bytes 2884
  160.1 57.3 %copy-start.23 = (f32[24,10]{0,1:T(8,128)S(1)}, f32[24,10]{0,1:T(8,128)}, u32[]{:S(2)}) copy-start(f32[24,10]{0,1:T(8,128)} %param.47) | copy-start | bytes 2884
